TPU v7x, 32 devices: a whole 2x2x4 slice. The times are simulated.
32 devices in a mesh: pop: 8 (over y, x, core), tp: 4 (over z).
Axes of the slice: x: 2, y: 2, z: 4, core: 2. Of those that a mesh axis runs over, the one named last changes fastest.
Arguments:
- tokens: bfloat16 [8, 256, 4096], P('pop', None, 'tp'), may hold values from -6 to 6
- receptance: bfloat16 [8, 256, 4096], P('pop', None, 'tp'), may hold values from -6 to 6
- keys: bfloat16 [8, 256, 4096], P('pop', None, 'tp'), may hold values from -0.29882812 to 0.29882812
- log_decay: bfloat16 [8, 256, 4096], P('pop', None, 'tp'), may hold values from -1 to 0
- value_weight: bfloat16 [4096, 4096], P('pop', 'tp'), may hold values from -0.09375 to 0.09375
- noise_in: bfloat16 [8, 4096], P('pop'), may hold values from -6 to 6
- noise_out: bfloat16 [8, 4096], P('pop', 'tp'), may hold values from -6 to 6
- utilities: float32 [8], P('pop'), may hold values from -0.5 to 0.5, as said below
- live_length: int32 [8], P('pop'), may hold values from 1 to 256, as said below
Outputs:
- wkv_out: bfloat16 [8, 256, 4096], P('pop', None, 'tp')
- update: float32 [4096, 4096], P('pop', 'tp')
Inputs may be any that keep to these rules, and one draw needn't show every extreme that they name: `utilities`: centered ranks: the values k / 7 - 0.5, each taken once. tokens at positions from live_length on are masked.
All inputs are finite; a program needn't handle non-finite values.
Results may differ from a plain program's by a relative error of at most 0.0049.
Values may be sent and summed in bfloat16 or wider, within the bound.
A program may use at most 128 MiB of HBM per device.

v0:
```python
import math

import jax
import jax.numpy as jnp
from jax import lax
from jax.sharding import PartitionSpec as P

HEAD = 64


HIGHEST = lax.Precision.HIGHEST
SIGMA = 0.5


def wkv_block(weighted_key_value_state, recept, masked_keys, masked_decay, value_items):
    cum_log = jnp.cumsum(masked_decay, axis=0)
    span_len = recept.shape[0]
    lower_mask = jnp.arange(span_len)[:, None] >= jnp.arange(span_len)[None, :]
    grown_recept = recept * jnp.exp(cum_log)
    shrunk_keys = masked_keys * jnp.exp(-cum_log)
    scores = jnp.where(lower_mask, jnp.dot(grown_recept, shrunk_keys.T, precision=HIGHEST), 0.0)
    block_out = jnp.dot(grown_recept, weighted_key_value_state, precision=HIGHEST) + jnp.dot(
        scores, value_items, precision=HIGHEST
    )
    final_log = cum_log[-1]
    carried = (masked_keys * jnp.exp(final_log[None, :] - cum_log)).T
    weighted_key_value_state = jnp.exp(final_log)[:, None] * weighted_key_value_state + jnp.dot(
        carried, value_items, precision=HIGHEST
    )
    return (weighted_key_value_state, block_out)


def body(
    tokens, receptance, keys, log_decay, value_weight, noise_in, noise_out, utilities, live_length
):
    members, length, local_width = receptance.shape
    all_features = lax.all_gather(tokens, "tp", axis=2, tiled=True)
    full_width = all_features.shape[2]
    flat_tokens = all_features.reshape(members * length, full_width)
    base_value = jnp.dot(
        flat_tokens,
        lax.all_gather(value_weight, "pop", axis=0, tiled=True),
        preferred_element_type=jnp.float32,
    )
    projected = jnp.einsum("mtd,md->mt", all_features, noise_in, preferred_element_type=jnp.float32)
    values = (
        base_value.reshape(members, length, local_width)
        + SIGMA
        / math.sqrt(full_width)
        * projected[:, :, None]
        * noise_out.astype(jnp.float32)[:, None, :]
    ).astype(jnp.bfloat16)
    live_mask = (jnp.arange(length)[None, :] < live_length[:, None]).astype(jnp.float32)
    head_count = local_width // HEAD

    def to_items(array_in):
        return (
            array_in.reshape(members, length, head_count, HEAD)
            .transpose(0, 2, 1, 3)
            .reshape(members * head_count, length, HEAD)
        )

    recept = to_items(receptance.astype(jnp.float32))
    masked_keys = to_items(keys.astype(jnp.float32) * live_mask[:, :, None])
    masked_decay = to_items(log_decay.astype(jnp.float32) * live_mask[:, :, None])
    value_items = to_items(values.astype(jnp.float32))
    block_len = min(32, length)
    weighted_key_value_state = jnp.zeros((members * head_count, HEAD, HEAD), jnp.float32)
    advance_tokens = jax.vmap(wkv_block)
    pieces = []
    for offset in range(0, length, block_len):
        operands = (
            weighted_key_value_state,
            recept[:, offset : offset + block_len],
            masked_keys[:, offset : offset + block_len],
            masked_decay[:, offset : offset + block_len],
            value_items[:, offset : offset + block_len],
        )
        weighted_key_value_state, block_out = advance_tokens(*operands)
        pieces.append(block_out)
    emitted_vector = jnp.concatenate(pieces, 1)
    emitted_vector = (
        emitted_vector.reshape(members, head_count, length, HEAD)
        .transpose(0, 2, 1, 3)
        .reshape(members, length, local_width)
    )
    wkv_out = (emitted_vector * live_mask[:, :, None]).astype(jnp.bfloat16)
    population = members * lax.axis_size("pop")
    weighted = noise_in.astype(jnp.float32) * (utilities / math.sqrt(population))[:, None]
    owned_rows = lax.all_to_all(weighted, "pop", split_axis=1, concat_axis=0, tiled=True)
    owned_columns = lax.all_gather(noise_out, "pop", axis=0, tiled=True)
    update = lax.dot_general(
        owned_rows,
        owned_columns.astype(jnp.float32),
        (((0,), (0,)), ((), ())),
        precision=HIGHEST,
        preferred_element_type=jnp.float32,
    )
    return (wkv_out, update)


def solution(mesh):
    return jax.shard_map(
        body,
        mesh=mesh,
        in_specs=(
            P("pop", None, "tp"),
            P("pop", None, "tp"),
            P("pop", None, "tp"),
            P("pop", None, "tp"),
            P("pop", "tp"),
            P("pop", None),
            P("pop", "tp"),
            P("pop"),
            P("pop"),
        ),
        out_specs=(P("pop", None, "tp"), P("pop", "tp")),
        check_vma=False,
    )
```

profile of v0, /device:TPU:1, one launch (start us, length us, event | category | flops | bytes accessed | tf_op | source)
XLA Modules:
  0.0 141.9 jit_solution(10558081617116915966)
XLA Ops:
  9.3 1.3 convert_multiply_fusion.2
  10.6 5.2 %all-to-all-start = ((f32[1,8,512]{2,0,1:T(1,128)}), f32[1,8,512]{2,0,1:T(1,128)S(1)}, u32[]{:S(2)}, u32[]{:S(2)}) async-start(f32[1,8,512]{2,0,1:T(1,128)} %bitcast.32), calls=%async_computation | async-start | bytes 32768 | tf_op jit(solution)/shard_map/all_to_all | solution.py:90
  16.5 2.0 %copy.57 = bf16[1,256,1024]{1,2,0:T(8,128)(2,1)} copy(bf16[1,256,1024]{2,1,0:T(8,128)(2,1)} %param.10) | data formatting | bytes 1048576 | tf_op args[1]
  19.2 2.5 %copy.63 = f32[1,256,16,64]{3,2,1,0:T(8,128)} copy(f32[1,256,16,64]{1,3,2,0:T(8,128)S(1)} %bitcast.121) | data formatting | bytes 2097152 | tf_op jit(solution)/shard_map/reshape | solution.py:58
  21.7 2.0 %copy.58 = f32[1,256,16,64]{3,2,1,0:T(8,128)S(1)} copy(bf16[1,256,16,64]{1,3,2,0:T(8,128)(2,1)} %bitcast.123) | data formatting | bytes 1572864 | tf_op jit(solution)/shard_map/reshape | solution.py:60
  23.7 2.8 %fusion.87 = (f32[16,32,64]{1,2,0:T(8,128)}, f32[16,32,64]{1,2,0:T(8,128)}, f32[16,32,64]{1,2,0:T(8,128)}, f32[16,32,64]{1,2,0:T(8,128)}, f32[16,32,64]{1,2,0:T(...) fusion(f32[16,256,64]{1,2,0:T(8,128)S(1)} %bitcast.102), kind=kLoop, calls=%fused_computation.144 | loop fusion | bytes 2097152 | tf_op jit(solution)/shard_map/slice | solution.py:76
  26.5 1.3 copy.98
  27.8 2.0 %copy.93 = f32[16,32,64]{2,0,1:T(8,128)} copy(f32[16,32,64]{1,2,0:T(8,128)} %get-tuple-element.41) | data formatting | bytes 262144 | tf_op jit(solution)/shard_map/slice | solution.py:76
  29.8 2.0 %copy.88 = f32[16,32,64]{2,0,1:T(8,128)} copy(f32[16,32,64]{1,2,0:T(8,128)} %get-tuple-element.42) | data formatting | bytes 262144 | tf_op jit(solution)/shard_map/slice | solution.py:76
  31.8 1.9 %copy.83 = f32[16,32,64]{2,0,1:T(8,128)} copy(f32[16,32,64]{1,2,0:T(8,128)} %get-tuple-element.43) | data formatting | bytes 262144 | tf_op jit(solution)/shard_map/slice | solution.py:76
  33.8 2.0 %copy.78 = f32[16,32,64]{2,0,1:T(8,128)} copy(f32[16,32,64]{1,2,0:T(8,128)} %get-tuple-element.44) | data formatting | bytes 262144 | tf_op jit(solution)/shard_map/slice | solution.py:76
  35.7 1.9 %copy.73 = f32[16,32,64]{2,0,1:T(8,128)} copy(f32[16,32,64]{1,2,0:T(8,128)} %get-tuple-element.45) | data formatting | bytes 262144 | tf_op jit(solution)/shard_map/slice | solution.py:76
  41.9 1.9 %fusion.92 = f32[16,32,64]{2,0,1:T(8,128)S(1)} fusion(f32[16,32,64]{2,0,1:T(8,128)S(1)} %copy-done.25), kind=kOutput, calls=%fused_computation.149 | output fusion | flops 1015808 | bytes 262144 | tf_op jit(solution)/shard_map/vmap(jit(cumsum))/reduce_window_sum | solution.py:16
  43.8 1.9 %fusion.90 = f32[16,32,64]{2,0,1:T(8,128)S(1)} fusion(f32[16,32,64]{2,0,1:T(8,128)S(1)} %copy-done.27), kind=kOutput, calls=%fused_computation.147 | output fusion | flops 1015808 | bytes 262144 | tf_op jit(solution)/shard_map/vmap(jit(cumsum))/reduce_window_sum | solution.py:16
  45.7 1.9 %fusion.89 = f32[16,32,64]{2,0,1:T(8,128)S(1)} fusion(f32[16,32,64]{2,0,1:T(8,128)S(1)} %copy-done.26), kind=kOutput, calls=%fused_computation.146 | output fusion | flops 1015808 | bytes 262144 | tf_op jit(solution)/shard_map/vmap(jit(cumsum))/reduce_window_sum | solution.py:16
  47.6 1.9 %fusion.88 = f32[16,32,64]{2,0,1:T(8,128)S(1)} fusion(f32[16,32,64]{2,0,1:T(8,128)S(1)} %copy.60), kind=kOutput, calls=%fused_computation.145 | output fusion | flops 1015808 | bytes 262144 | tf_op jit(solution)/shard_map/vmap(jit(cumsum))/reduce_window_sum | solution.py:16
  49.5 1.9 %fusion.95 = f32[16,32,64]{2,0,1:T(8,128)S(1)} fusion(f32[16,32,64]{2,0,1:T(8,128)S(1)} %copy.98), kind=kOutput, calls=%fused_computation.152 | output fusion | flops 1015808 | bytes 262144 | tf_op jit(solution)/shard_map/vmap(jit(cumsum))/reduce_window_sum | solution.py:16
  51.9 1.1 fusion.34
  54.6 1.4 convolution_select_fusion.7
  57.0 1.4 convolution_select_fusion.2
  58.3 1.4 convolution_select_fusion.6
  59.7 1.4 convolution_select_fusion.5
  61.1 1.4 convolution_select_fusion.4
  62.5 1.4 convolution_select_fusion.3
  63.9 1.4 convolution_select_fusion.1
  65.3 1.4 convolution_select_fusion
  66.7 9.7 %all-gather = bf16[8,1,1024]{2,1,0:T(2,128)(2,1)S(1)} all-gather(bf16[1,1,1024]{2,1,0:T(2,128)(2,1)S(1)} %bitcast.125), channel_id=1, replica_groups=mesh['pop'=8,'tp'=4] {'pop'}, dimensions={0}, use_global_device_ids=true | all-gather | bytes 18432 | tf_op jit(solution)/shard_map/all_gather | solution.py:91
  76.4 2.4 %fusion.74 = f32[512,1024]{1,0:T(8,128)} fusion(bf16[8,1,1024]{2,1,0:T(2,128)(2,1)S(1)} %all-gather, f32[1,8,512]{2,0,1:T(1,128)S(1)} %all-to-all-done), kind=kOutput, calls=%fused_computation.119 | convolution fusion | flops 50331648 | bytes 2129920 | tf_op jit(solution)/shard_map/dot_general | solution.py:92
  78.8 2.4 %fusion = f32[1,256]{1,0:T(1,128)S(1)} fusion(bf16[1,256,4096]{2,1,0:T(8,128)(2,1)} %all-gather.4.cloned.1.call-done, bf16[1,4096]{1,0:T(2,128)(2,1)S(1)} %copy-done.33), kind=kOutput, calls=%fused_computation | convolution fusion | flops 2097152 | bytes 2106368 | tf_op jit(solution)/shard_map/mtd,md->mt/dot_general | solution.py:45
  81.2 32.0 %all-gather.6.cloned.1.call-done = bf16[4096,1024]{1,0:T(8,128)(2,1)} async-done(((bf16[512,1024]{1,0:T(8,128)(2,1)}), bf16[4096,1024]{1,0:T(8,128)(2,1)}) %all-gather.6.cloned.1.call-update) | async-done | bytes 8388624 | tf_op jit(solution)/shard_map/all_gather | solution.py:42
  113.2 6.5 %fusion.7 = bf16[256,1024]{1,0:T(8,128)(2,1)} fusion(bf16[4096,1024]{1,0:T(8,128)(2,1)} %all-gather.6.cloned.1.call-done, bf16[1,256,4096]{2,1,0:T(8,128)(2,1)S(1)} %copy-done.15, f32[1024]{0:T(1024)S(1)} %bitcast.127, f32[256]{0:T(256)S(1)} %broadcast_multiply_fusion), kind=kOutput, calls=%fused_computation.5 | convolution fusion | flops 2148270080 | bytes 11015168 | tf_op jit(solution)/shard_map/dot_general | solution.py:40
  119.7 1.3 copy.66
  (128 shorter events, 22.8 us)
Async XLA Ops:
  7.2 11.4 %copy-start.31 = (bf16[1,256,1024]{2,1,0:T(8,128)(2,1)S(1)}, bf16[1,256,1024]{2,1,0:T(8,128)(2,1)}, u32[]{:S(2)}) copy-start(bf16[1,256,1024]{2,1,0:T(8,128)(2,1)} %param.11) | copy-start | bytes 1572868
  7.2 11.6 %copy-start.32 = (bf16[1,256,1024]{2,1,0:T(8,128)(2,1)S(1)}, bf16[1,256,1024]{2,1,0:T(8,128)(2,1)}, u32[]{:S(2)}) copy-start(bf16[1,256,1024]{2,1,0:T(8,128)(2,1)} %param.12) | copy-start | bytes 1572868
  7.2 71.6 %all-gather.4.cloned.1.call-start = ((), (), s32[]{:S(2)}) async-start(), calls=%async_computation.1 | async-start | bytes 2621440 | tf_op jit(solution)/shard_map/all_gather | solution.py:37
  7.9 105.3 %all-gather.6.cloned.1.call-start = ((), (), s32[]{:S(2)}) async-start(), calls=%async_computation.2 | async-start | bytes 9437184 | tf_op jit(solution)/shard_map/all_gather | solution.py:42
  10.6 65.8 %all-to-all-start = ((f32[1,8,512]{2,0,1:T(1,128)}), f32[1,8,512]{2,0,1:T(1,128)S(1)}, u32[]{:S(2)}, u32[]{:S(2)}) async-start(f32[1,8,512]{2,0,1:T(1,128)} %bitcast.32), calls=%async_computation | async-start | bytes 32768 | tf_op jit(solution)/shard_map/all_to_all | solution.py:90
  27.8 9.9 %copy-start.14 = (f32[16,32,64]{1,2,0:T(8,128)S(1)}, f32[16,32,64]{1,2,0:T(8,128)}, u32[]{:S(2)}) copy-start(f32[16,32,64]{1,2,0:T(8,128)} %get-tuple-element.46) | copy-start | bytes 393220
  29.8 8.8 %copy-start.13 = (f32[16,32,64]{1,2,0:T(8,128)S(1)}, f32[16,32,64]{1,2,0:T(8,128)}, u32[]{:S(2)}) copy-start(f32[16,32,64]{1,2,0:T(8,128)} %get-tuple-element.47) | copy-start | bytes 393220
  38.6 3.3 %copy-start.25 = (f32[16,32,64]{2,0,1:T(8,128)S(1)}, f32[16,32,64]{2,0,1:T(8,128)}, u32[]{:S(2)}) copy-start(f32[16,32,64]{2,0,1:T(8,128)} %copy.83) | copy-start | bytes 393220
  38.8 5.0 %copy-start.27 = (f32[16,32,64]{2,0,1:T(8,128)S(1)}, f32[16,32,64]{2,0,1:T(8,128)}, u32[]{:S(2)}) copy-start(f32[16,32,64]{2,0,1:T(8,128)} %copy.73) | copy-start | bytes 393220
  38.8 6.9 %copy-start.26 = (f32[16,32,64]{2,0,1:T(8,128)S(1)}, f32[16,32,64]{2,0,1:T(8,128)}, u32[]{:S(2)}) copy-start(f32[16,32,64]{2,0,1:T(8,128)} %copy.68) | copy-start | bytes 393220
  51.4 2.1 %copy-start = (f32[1,256,16,64]{3,2,1,0:T(8,128)S(1)}, f32[1,256,16,64]{3,2,1,0:T(8,128)}, u32[]{:S(2)}) copy-start(f32[1,256,16,64]{3,2,1,0:T(8,128)} %copy.63) | copy-start | bytes 3145732
  51.8 5.1 %copy-start.3 = (f32[16,32,64]{2,0,1:T(8,128)}, f32[16,32,64]{2,0,1:T(8,128)S(1)}, u32[]{:S(2)}) copy-start(f32[16,32,64]{2,0,1:T(8,128)S(1)} %get-tuple-element.23) | copy-start | bytes 393220
  51.8 6.5 %copy-start.11 = (f32[16,32,64]{2,0,1:T(8,128)}, f32[16,32,64]{2,0,1:T(8,128)S(1)}, u32[]{:S(2)}) copy-start(f32[16,32,64]{2,0,1:T(8,128)S(1)} %get-tuple-element.27) | copy-start | bytes 393220
  51.8 7.9 %copy-start.9 = (f32[16,32,64]{2,0,1:T(8,128)}, f32[16,32,64]{2,0,1:T(8,128)S(1)}, u32[]{:S(2)}) copy-start(f32[16,32,64]{2,0,1:T(8,128)S(1)} %get-tuple-element.26) | copy-start | bytes 393220
  51.9 9.3 %copy-start.7 = (f32[16,32,64]{2,0,1:T(8,128)}, f32[16,32,64]{2,0,1:T(8,128)S(1)}, u32[]{:S(2)}) copy-start(f32[16,32,64]{2,0,1:T(8,128)S(1)} %get-tuple-element.25) | copy-start | bytes 393220
  51.9 10.6 %copy-start.5 = (f32[16,32,64]{2,0,1:T(8,128)}, f32[16,32,64]{2,0,1:T(8,128)S(1)}, u32[]{:S(2)}) copy-start(f32[16,32,64]{2,0,1:T(8,128)S(1)} %get-tuple-element.24) | copy-start | bytes 393220
  51.9 12.0 %copy-start.1 = (f32[16,32,64]{2,0,1:T(8,128)}, f32[16,32,64]{2,0,1:T(8,128)S(1)}, u32[]{:S(2)}) copy-start(f32[16,32,64]{2,0,1:T(8,128)S(1)} %get-tuple-element.22) | copy-start | bytes 393220
  59.7 7.0 %copy-start.34 = (bf16[1,1024]{1,0:T(2,128)(2,1)S(1)}, bf16[1,1024]{1,0:T(2,128)(2,1)}, u32[]{:S(2)}) copy-start(bf16[1,1024]{1,0:T(2,128)(2,1)} %param.15) | copy-start | bytes 6148
  62.5 16.3 %copy-start.33 = (bf16[1,4096]{1,0:T(2,128)(2,1)S(1)}, bf16[1,4096]{1,0:T(2,128)(2,1)}, u32[]{:S(2)}) copy-start(bf16[1,4096]{1,0:T(2,128)(2,1)} %param.14) | copy-start | bytes 24580
  78.8 34.4 %copy-start.15 = (bf16[1,256,4096]{2,1,0:T(8,128)(2,1)S(1)}, bf16[1,256,4096]{2,1,0:T(8,128)(2,1)}, u32[]{:S(2)}) copy-start(bf16[1,256,4096]{2,1,0:T(8,128)(2,1)} %all-gather.4.cloned.1.call-done) | copy-start | bytes 6291460
  119.7 2.4 %copy-start.12 = (f32[16,32,64]{2,0,1:T(8,128)S(1)}, f32[16,32,64]{2,0,1:T(8,128)}, u32[]{:S(2)}) copy-start(f32[16,32,64]{2,0,1:T(8,128)} %copy-done.11) | copy-start | bytes 393220
  119.7 3.2 %copy-start.28 = (f32[16,32,64]{2,0,1:T(8,128)S(1)}, f32[16,32,64]{2,0,1:T(8,128)}, u32[]{:S(2)}) copy-start(f32[16,32,64]{2,0,1:T(8,128)} %get-tuple-element.33) | copy-start | bytes 393220
  121.5 2.0 %copy-start.10 = (f32[16,32,64]{2,0,1:T(8,128)S(1)}, f32[16,32,64]{2,0,1:T(8,128)}, u32[]{:S(2)}) copy-start(f32[16,32,64]{2,0,1:T(8,128)} %copy-done.9) | copy-start | bytes 393220
  122.8 2.0 %copy-start.8 = (f32[16,32,64]{2,0,1:T(8,128)S(1)}, f32[16,32,64]{2,0,1:T(8,128)}, u32[]{:S(2)}) copy-start(f32[16,32,64]{2,0,1:T(8,128)} %copy-done.7) | copy-start | bytes 393220
  123.5 2.0 %copy-start.30 = (f32[16,32,64]{2,0,1:T(8,128)S(1)}, f32[16,32,64]{2,0,1:T(8,128)}, u32[]{:S(2)}) copy-start(f32[16,32,64]{2,0,1:T(8,128)} %get-tuple-element.37) | copy-start | bytes 393220
  124.2 2.0 %copy-start.6 = (f32[16,32,64]{2,0,1:T(8,128)S(1)}, f32[16,32,64]{2,0,1:T(8,128)}, u32[]{:S(2)}) copy-start(f32[16,32,64]{2,0,1:T(8,128)} %copy-done.5) | copy-start | bytes 393220
  124.8 2.0 %copy-start.29 = (f32[16,32,64]{2,0,1:T(8,128)S(1)}, f32[16,32,64]{2,0,1:T(8,128)}, u32[]{:S(2)}) copy-start(f32[16,32,64]{2,0,1:T(8,128)} %get-tuple-element.39) | copy-start | bytes 393220
  125.5 2.0 %copy-start.4 = (f32[16,32,64]{2,0,1:T(8,128)S(1)}, f32[16,32,64]{2,0,1:T(8,128)}, u32[]{:S(2)}) copy-start(f32[16,32,64]{2,0,1:T(8,128)} %copy-done.3) | copy-start | bytes 393220
  128.9 2.3 %copy-start.16 = (f32[16,32,32]{2,1,0:T(8,128)S(1)}, f32[16,32,32]{2,1,0:T(8,128)}, u32[]{:S(2)}) copy-start(f32[16,32,32]{2,1,0:T(8,128)} %convolution_select_fusion.7) | copy-start | bytes 196612
  128.9 2.3 %copy-start.24 = (f32[16,32,64]{2,1,0:T(8,128)S(1)}, f32[16,32,64]{2,1,0:T(8,128)}, u32[]{:S(2)}) copy-start(f32[16,32,64]{2,1,0:T(8,128)} %fusion.34) | copy-start | bytes 393220
  128.9 2.5 %copy-start.23 = (f32[16,32,32]{2,1,0:T(8,128)S(1)}, f32[16,32,32]{2,1,0:T(8,128)}, u32[]{:S(2)}) copy-start(f32[16,32,32]{2,1,0:T(8,128)} %convolution_select_fusion.6) | copy-start | bytes 196612
  129.6 2.2 %copy-start.22 = (f32[16,32,32]{2,1,0:T(8,128)S(1)}, f32[16,32,32]{2,1,0:T(8,128)}, u32[]{:S(2)}) copy-start(f32[16,32,32]{2,1,0:T(8,128)} %convolution_select_fusion.5) | copy-start | bytes 196612
  (6 other events, 8.7 us)
Sparse Core Ops, SparseCore 0:
  9.6 47.9 all-gather.3
  59.5 53.6 all-gather.5
where the time goes:
time: 143 us; the launch traced here: 142 us
  matrix products  34.8 us (24%)
  waiting for transfers between devices  33.4 us (23%)
  local copies, waits for them, and re-layouts  26.1 us (18%)
  other arithmetic  16.5 us (12%)
  between operations  16.1 us (11%)
  blocking collectives  9.7 us (7%)
  starting transfers between devices  5.3 us (4%)
    all_gather x1, waiting for transfers between devices, body(): lax.all_gather(value_weight, 'pop', axis=0, tiled=True)  32 us
    slice x9, local copies, waits for them, and re-layouts, body(): masked_decay[:, offset:offset + block_len]  15.1 us
    another operation x8, other arithmetic, wkv_block(): cum_log = jnp.cumsum(masked_decay, axis=0)  12.4 us
    dot_general x8, matrix products, wkv_block(): jnp.dot(grown_recept, shrunk_keys.T, precision=HIGHEST)  11.1 us
    all_gather x1, blocking collectives, body(): owned_columns = lax.all_gather(noise_out, 'pop', axis=0, tiled=True)  9.7 us
    dot_general x1, matrix products, body(): jnp.dot(flat_tokens, lax.all_gather(value_weight, 'pop', axis=0, tiled=Tr...  6.51 us
    dot_general x8, matrix products, wkv_block(): jnp.dot(grown_recept, weighted_key_value_state, precision=HIGHEST)  5.77 us
    all_to_all x1, starting transfers between devices, body(): lax.all_to_all(weighted, 'pop', split_axis=1, concat_axis=0, tiled=True)  5.22 us
  transfers between devices with their start and end apart: 3, of which 1 were waited for; matrix products, arithmetic and copies ran while one was open for 39% of the time, Pallas kernels for 0%

commit v1 on v0

v1 whole, which is shorter than its diff:
```python
import functools
import math

import jax
import jax.numpy as jnp
from jax import lax
from jax.experimental import pallas as pl
from jax.experimental.pallas import tpu as pltpu
from jax.sharding import PartitionSpec as P

HEAD = 64
SIGMA = 0.5
LANES = 128
WCUTS = 4
TCUTS = 2
MESH = pl.DeviceIdType.MESH
F32 = jnp.float32
BF16 = jnp.bfloat16


def dot_nt(a, b):
    return lax.dot_general(a, b, (((1,), (1,)), ((), ())), preferred_element_type=F32)


def dot_nn(a, b):
    return jnp.dot(a, b, preferred_element_type=F32)


def flip(index, bit):
    return index + bit - 2 * bit * lax.rem(lax.div(index, bit), 2)


def kernel(
    pop,
    tp,
    tok,
    rec,
    key,
    dec,
    w,
    nin,
    nout,
    util,
    live,
    wkv,
    upd,
    tok_buf,
    wbuf,
    s_low,
    s_high,
    proj,
    small_src,
    small_dst,
    upd_buf,
    own_sem,
    upd_sem,
    small_send,
    small_recv,
    group_send,
    group_recv,
    x_send,
    x_recv,
    y_send,
    y_recv,
    c_send,
    c_recv,
    dn_send,
    dn_recv,
    up_send,
    up_recv,
):
    length, width = rec.shape[1], rec.shape[2]
    full = tp * width
    rows = w.shape[0]
    group = pop // 8
    block = rows * group
    cut = block // WCUTS
    tcut = length // TCUTS
    win = upd_buf.shape[0]
    half = length // 2

    p = lax.axis_index("pop")
    k = lax.axis_index("tp")
    q = lax.div(p, group)
    place = lax.rem(p, group)

    def remote(src, dst, send, recv, **where):
        return pltpu.make_async_remote_copy(
            src_ref=src, dst_ref=dst, send_sem=send, recv_sem=recv, device_id=where, device_id_type=MESH
        )

    barrier = pltpu.get_barrier_semaphore()
    for d in range(1, pop):
        pl.semaphore_signal(barrier, inc=1, device_id={"pop": lax.rem(p + d, pop)}, device_id_type=MESH)

    @pl.when(k >= 1)
    def _():
        pl.semaphore_signal(barrier, inc=1, device_id={"tp": k - 1}, device_id_type=MESH)

    @pl.when(k <= tp - 2)
    def _():
        pl.semaphore_signal(barrier, inc=1, device_id={"tp": k + 1}, device_id_type=MESH)

    own_tok = pltpu.make_async_copy(tok.at[0], tok_buf.at[k], own_sem.at[0])
    own_w = pltpu.make_async_copy(w, wbuf.at[pl.ds(pl.multiple_of(p * rows, rows), rows)], own_sem.at[1])
    own_tok.start()
    own_w.start()

    scale = util[0] * (1.0 / math.sqrt(pop))
    weighted = nin[...].astype(F32) * scale
    out_factor = nout[...].astype(F32)
    for dest in range(pop):
        start = dest * rows // LANES * LANES
        small_src[dest, :, 0:win] = weighted[:, start : start + win]
        small_src[dest, :, win : win + width] = out_factor
    neighbours = jnp.where(k >= 1, 1, 0) + jnp.where(k <= tp - 2, 1, 0)
    pl.semaphore_wait(barrier, pop - 1 + neighbours)

    sent = []

    def tok_rows(index, c):
        return tok_buf.at[index, pl.ds(c * tcut, tcut)]

    def down(s, c):
        src = tok.at[0, pl.ds(c * tcut, tcut)] if s == 0 else tok_rows(k + s, c)
        return remote(src, tok_rows(k + s, c), dn_send.at[s, c], dn_recv.at[s, c], tp=k - 1)

    def up(s, c):
        src = tok.at[0, pl.ds(c * tcut, tcut)] if s == 0 else tok_rows(k - s, c)
        return remote(src, tok_rows(k - s, c), up_send.at[s, c], up_recv.at[s, c], tp=k + 1)

    def down_sends(s):
        return (k >= 1) & (k + s <= tp - 1)

    def up_sends(s):
        return (k <= tp - 2) & (k - s >= 0)

    def start_tokens(s, c):
        @pl.when(down_sends(s))
        def _():
            down(s, c).start()

        @pl.when(up_sends(s))
        def _():
            up(s, c).start()

    def take_tokens(s, c):
        @pl.when(k + 1 + s <= tp - 1)
        def _():
            landed = tok_rows(k + 1 + s, c)
            remote(landed, landed, dn_send.at[s, c], dn_recv.at[s, c], tp=k).wait_recv()

        @pl.when(k - 1 - s >= 0)
        def _():
            landed = tok_rows(k - 1 - s, c)
            remote(landed, landed, up_send.at[s, c], up_recv.at[s, c], tp=k).wait_recv()

        if s + 1 <= tp - 2:
            start_tokens(s + 1, c)

    qx, qy, qc = flip(q, 2), flip(q, 4), flip(q, 1)
    qd = flip(qx, 4)

    def piece(index, c):
        return wbuf.at[pl.ds(pl.multiple_of(index * block + c * cut, cut), cut)]

    def own_piece(c):
        return w.at[pl.ds(c * cut, cut)] if group == 1 else piece(q, c)

    def send(src, dst, sems, recvs, slot, target):
        copy = remote(src, dst, sems.at[slot], recvs.at[slot], pop=target * group + place)
        copy.start()
        sent.append(copy)

    def landed(index, c, recvs, slot):
        here = piece(index, c)
        remote(here, here, x_send.at[0], recvs.at[slot], pop=p).wait_recv()

    for c in range(TCUTS):
        start_tokens(0, c)

    if group > 1:
        mine = wbuf.at[pl.ds(pl.multiple_of(p * rows, rows), rows)]
        for d in range(1, group):
            target = q * group + lax.rem(place + d, group)
            copy = remote(w, mine, group_send.at[d - 1], group_recv.at[d - 1], pop=target)
            copy.start()
            sent.append(copy)
        own_w.wait()
        for d in range(1, group):
            origin = q * group + lax.rem(place + group - d, group)
            here = wbuf.at[pl.ds(pl.multiple_of(origin * rows, rows), rows)]
            remote(here, here, group_send.at[d - 1], group_recv.at[d - 1], pop=p).wait_recv()

    x_order = list(range(WCUTS))
    y_order = x_order[WCUTS // 2 :] + x_order[: WCUTS // 2]
    for i in range(WCUTS):
        send(own_piece(x_order[i]), piece(q, x_order[i]), x_send, x_recv, x_order[i], qx)
        send(own_piece(y_order[i]), piece(q, y_order[i]), y_send, y_recv, y_order[i], qy)
        if i == 0:
            for d in range(1, pop):
                target = lax.rem(p + d, pop)
                copy = remote(
                    small_src.at[target], small_dst.at[p], small_send.at[d - 1], small_recv.at[d - 1], pop=target
                )
                copy.start()
                sent.append(copy)
    for i in range(WCUTS):
        send(own_piece(i), piece(q, i), c_send, c_recv, i, qc)
    small_dst[p] = small_src[p]

    def round_of(i):
        if i < WCUTS:
            cx, cy = x_order[i], y_order[i]
            landed(qx, cx, x_recv, cx)
            if i < WCUTS // 2:
                send(piece(qx, cx), piece(qx, cx), y_send, y_recv, WCUTS + i, qy)
            send(piece(qx, cx), piece(qx, cx), c_send, c_recv, WCUTS + cx, qc)
            landed(qy, cy, y_recv, cy)
            if i < WCUTS // 2:
                send(piece(qy, cy), piece(qy, cy), x_send, x_recv, WCUTS + i, qx)
            send(piece(qy, cy), piece(qy, cy), c_send, c_recv, 2 * WCUTS + cy, qc)
        else:
            cx, cy = y_order[i - WCUTS], x_order[i - WCUTS]
            landed(qd, cx, x_recv, i)
            send(piece(qd, cx), piece(qd, cx), c_send, c_recv, 3 * WCUTS + cx, qc)
            landed(qd, cy, y_recv, i)
            send(piece(qd, cy), piece(qd, cy), c_send, c_recv, 3 * WCUTS + cy, qc)

    live_count = live[0]
    lane = lax.broadcasted_iota(jnp.int32, (half, LANES), 1)
    first = (lane < HEAD).astype(F32)
    second = 1.0 - first
    row = lax.broadcasted_iota(jnp.int32, (half, LANES), 0)
    masks = []
    span = 32
    col = lax.broadcasted_iota(jnp.int32, (half, half), 1)
    prow = lax.broadcasted_iota(jnp.int32, (half, half), 0)
    row_block, col_block = lax.div(prow, span), lax.div(col, span)
    diag_mask = (row_block == col_block) & (col <= prow)
    near_mask = (lax.rem(row_block, 2) == 1) & (col_block == row_block - 1)
    far_mask = (row_block >= 2) & (col_block < 2)
    lower = (
        lax.broadcasted_iota(jnp.int32, (length, length), 0) >= lax.broadcasted_iota(jnp.int32, (length, length), 1)
    ).astype(BF16)

    def spread(cum, at, count):
        return jnp.concatenate([jnp.broadcast_to(cum[a : a + 1], (count, LANES)) for a in at], 0)

    def heads_of(queries):
        return jnp.concatenate([queries * first, queries * second], 0).astype(BF16)

    def scores_of(index):
        lanes = pl.ds(pl.multiple_of(index * LANES, LANES), LANES)
        t = lax.broadcasted_iota(jnp.int32, (length, LANES), 0)
        mask = (t < live_count).astype(F32)
        recept = rec[0, :, lanes].astype(F32) * mask
        keys = key[0, :, lanes].astype(F32) * mask
        decay = (dec[0, :, lanes].astype(F32) * mask).astype(BF16)
        cum = dot_nn(lower, decay)
        fade = jnp.exp(-jnp.abs(cum - cum[half - 1 : half]))
        cross = dot_nt(heads_of(recept[half:] * fade[half:]), (keys[:half] * fade[:half]).astype(BF16))
        far = jnp.exp(-jnp.abs(cum - spread(cum, (63, 191), half)))
        near = jnp.exp(-jnp.abs(cum - spread(cum, (31, 95, 159, 223), 64)))
        inner = cum - spread(cum, tuple(range(15, length, span)), span)
        grow, shrink = jnp.exp(inner), jnp.exp(-inner)
        out = []
        for h in range(2):
            part = slice(h * half, (h + 1) * half)
            r, kk = recept[part], keys[part]
            far_s = dot_nt(heads_of(r * far[part]), (kk * far[part]).astype(BF16))
            near_s = dot_nt(heads_of(r * near[part]), (kk * near[part]).astype(BF16))
            diag_s = dot_nt(heads_of(r * grow[part]), (kk * shrink[part]).astype(BF16))
            for a in range(2):
                sel = slice(a * half, (a + 1) * half)
                out.append(
                    jnp.where(
                        diag_mask, diag_s[sel], jnp.where(near_mask, near_s[sel], jnp.where(far_mask, far_s[sel], 0.0))
                    ).astype(BF16)
                )
        cross = cross.astype(BF16)
        s_low[index, :, 0:half] = out[0]
        s_low[index, :, half : 2 * half] = out[1]
        s_high[index, :, 0:half] = cross[:half]
        s_high[index, :, half : 2 * half] = out[2]
        s_high[index, :, 2 * half : 3 * half] = cross[half:]
        s_high[index, :, 3 * half : 4 * half] = out[3]

    pairs = width // LANES
    done = 0

    def score_pairs(begin, end):
        @pl.loop(begin, end)
        def _(index):
            scores_of(index)

    def update_part():
        for d in range(1, pop):
            origin = lax.rem(p + pop - d, pop)
            here = small_dst.at[origin]
            remote(here, here, small_send.at[d - 1], small_recv.at[d - 1], pop=p).wait_recv()
        factor = jnp.concatenate([small_dst[m, :, 0:win] for m in range(pop)], 0)
        high = factor.astype(BF16).astype(F32)
        mid = (factor - high).astype(BF16).astype(F32)
        low = factor - high - mid
        left = jnp.concatenate([high, mid, low], 0).T.astype(BF16)
        for n in range(0, width, 256):
            right = jnp.concatenate([small_dst[m, :, win + n : win + n + 256] for m in range(pop)], 0)
            right = jnp.concatenate([right, right, right], 0).astype(BF16)
            upd_buf[:, n : n + 256] = dot_nn(left, right)

    offset = pl.multiple_of(lax.rem(p * rows, LANES) if rows < LANES else 0, 8)
    upd_copy = pltpu.make_async_copy(upd_buf.at[pl.ds(offset, rows)], upd, upd_sem)

    rounds = WCUTS + WCUTS // 2
    bounds = [pairs * (i + 1) // rounds for i in range(rounds)]
    for i in range(rounds):
        score_pairs(done, bounds[i])
        done = bounds[i]
        round_of(i)
        if i == 1:
            update_part()
            upd_copy.start()
        step, c = divmod(i, TCUTS)
        if step <= tp - 2:
            take_tokens(step, c)

    own_tok.wait()
    for b, index in enumerate((qc, flip(qx, 1), flip(qy, 1), flip(qd, 1))):
        for c in range(WCUTS):
            landed(index, c, c_recv, b * WCUTS + c)
    if group == 1:
        own_w.wait()

    total = jnp.zeros((length, LANES), F32)
    for j in range(tp):
        part = jnp.broadcast_to(nin[:, j * width : (j + 1) * width].astype(F32), (LANES, width)).astype(BF16)
        total = total + dot_nt(tok_buf[j], part)
    proj[...] = total * (SIGMA / math.sqrt(full))

    tile = 2 * LANES

    @pl.loop(0, width // tile)
    def _(n):
        lanes = pl.ds(pl.multiple_of(n * tile, tile), tile)
        base = jnp.concatenate([proj[...], proj[...]], 1) * nout[:, lanes].astype(F32)
        for j in range(tp):
            base = base + dot_nn(tok_buf[j], wbuf[j * width : (j + 1) * width, lanes])
        values = base.astype(BF16)
        for b in range(2):
            pair = values[:, b * LANES : (b + 1) * LANES].astype(F32)
            head_a = jnp.concatenate([pair[:half] * first, pair[half:] * first], 0).astype(BF16)
            head_b = jnp.concatenate([pair[:half] * second, pair[half:] * second], 0).astype(BF16)
            index = n * 2 + b
            low_v = jnp.concatenate([head_a[:half], head_b[:half]], 0)
            high_v = jnp.concatenate([head_a, head_b], 0)
            here = pl.ds(pl.multiple_of(index * LANES, LANES), LANES)
            wkv[0, 0:half, here] = dot_nn(s_low[index], low_v).astype(BF16)
            wkv[0, half:length, here] = dot_nn(s_high[index], high_v).astype(BF16)

    for copy in sent:
        copy.wait_send()
    for s in range(tp - 1):
        for c in range(TCUTS):

            @pl.when(down_sends(s))
            def _():
                down(s, c).wait_send()

            @pl.when(up_sends(s))
            def _():
                up(s, c).wait_send()

    upd_copy.wait()


def body(pop, tp, tokens, receptance, keys, log_decay, value_weight, noise_in, noise_out, utilities, live_length):
    length, width = receptance.shape[1:]
    rows = value_weight.shape[0]
    full = rows * pop
    win = max(rows, LANES)
    pairs = width // LANES
    half = length // 2
    group = pop // 8
    dma = pltpu.SemaphoreType.DMA
    whole = pl.BlockSpec(memory_space=pltpu.VMEM)
    scalar = pl.BlockSpec(memory_space=pltpu.SMEM)
    anywhere = pl.BlockSpec(memory_space=pl.ANY)
    return pl.pallas_call(
        functools.partial(kernel, pop, tp),
        out_shape=(
            jax.ShapeDtypeStruct((1, length, width), BF16),
            jax.ShapeDtypeStruct((rows, width), F32),
        ),
        in_specs=[anywhere, whole, whole, whole, anywhere, whole, whole, scalar, scalar],
        out_specs=(whole, anywhere),
        scratch_shapes=[
            pltpu.VMEM((tp, length, width), BF16),
            pltpu.VMEM((full, width), BF16),
            pltpu.VMEM((pairs, half, 2 * half), BF16),
            pltpu.VMEM((pairs, half, 4 * half), BF16),
            pltpu.VMEM((length, LANES), F32),
            pltpu.VMEM((pop, 1, win + width), F32),
            pltpu.VMEM((pop, 1, win + width), F32),
            pltpu.VMEM((win, width), F32),
            dma((2,)),
            dma,
            dma((pop - 1,)),
            dma((pop - 1,)),
            dma((max(group - 1, 1),)),
            dma((max(group - 1, 1),)),
            dma((2 * WCUTS,)),
            dma((2 * WCUTS,)),
            dma((2 * WCUTS,)),
            dma((2 * WCUTS,)),
            dma((4 * WCUTS,)),
            dma((4 * WCUTS,)),
            dma((tp - 1, TCUTS)),
            dma((tp - 1, TCUTS)),
            dma((tp - 1, TCUTS)),
            dma((tp - 1, TCUTS)),
        ],
        compiler_params=pltpu.CompilerParams(
            collective_id=0, has_side_effects=True, vmem_limit_bytes=48 * 1024 * 1024
        ),
        cost_estimate=pl.CostEstimate(
            flops=2 * length * full * width, bytes_accessed=16 * 1024 * 1024, transcendentals=5 * length * width
        ),
    )(tokens, receptance, keys, log_decay, value_weight, noise_in, noise_out, utilities, live_length)


def solution(mesh):
    return jax.shard_map(
        functools.partial(body, mesh.shape["pop"], mesh.shape["tp"]),
        mesh=mesh,
        in_specs=(
            P("pop", None, "tp"),
            P("pop", None, "tp"),
            P("pop", None, "tp"),
            P("pop", None, "tp"),
            P("pop", "tp"),
            P("pop", None),
            P("pop", "tp"),
            P("pop"),
            P("pop"),
        ),
        out_specs=(P("pop", None, "tp"), P("pop", "tp")),
        check_vma=False,
    )
```

time: 143 us -> 58.7 us (0.41)
  Pallas kernels: 0 us -> 47.4 us
  matrix products: 34.8 us -> 0 us
  waiting for transfers between devices: 33.4 us -> 0 us
  local copies, waits for them, and re-layouts: 26.1 us -> 8.9 us
  other arithmetic: 16.5 us -> 0 us
  between operations: 16.1 us -> 1.95 us
  blocking collectives: 9.7 us -> 0 us
  starting transfers between devices: 5.3 us -> 0 us
    pallas_call x0 -> x1, Pallas kernels: none -> 47.4 us  [body(): pl.pallas_call(functools.partial(kernel, pop, tp), out_shape=(jax.ShapeDt...]
    dot_general x34 -> x0, matrix products: 34.8 us -> none  [the longest x8 11.1 us: wkv_block(): jnp.dot(grown_recept, shrunk_keys.T, precision=HIGHEST)]
    all_gather x2 -> x0, waiting for transfers between devices: 32 us -> none  [the longest x1 32 us: body(): lax.all_gather(value_weight, 'pop', axis=0, tiled=True)]
    slice x9 -> x0, local copies, waits for them, and re-layouts: 15.1 us -> none  [body(): masked_decay[:, offset:offset + block_len]]
    another operation x8 -> x0, other arithmetic: 12.4 us -> none  [wkv_block(): cum_log = jnp.cumsum(masked_decay, axis=0)]
    all_gather x1 -> x0, blocking collectives: 9.7 us -> none  [body(): owned_columns = lax.all_gather(noise_out, 'pop', axis=0, tiled=True)]
    all_to_all x1 -> x0, starting transfers between devices: 5.22 us -> none  [body(): lax.all_to_all(weighted, 'pop', split_axis=1, concat_axis=0, tiled=True)]
    reshape x3 -> x0, local copies, waits for them, and re-layouts: 4.96 us -> none  [the longest x2 2.95 us: to_items(): array_in.reshape(members, length, head_count, HEAD).transpose(0, 2, 1, 3)]
  transfers between devices with their start and end apart: 3 -> 0, of which waited for: 1 -> 0; matrix products, arithmetic and copies ran while one was open for 39% -> 0% of each run, Pallas kernels for 0% -> 0%
where the time goes in v1:
time: 58.7 us; the launch traced here: 58.3 us
  Pallas kernels  47.4 us (81%)
  local copies, waits for them, and re-layouts  8.9 us (15%)
  between operations  1.95 us (3%)
    pallas_call x1, Pallas kernels, body(): pl.pallas_call(functools.partial(kernel, pop, tp), out_shape=(jax.ShapeDt...  47.4 us
    unnamed x16, local copies, waits for them, and re-layouts  8.9 us

profile of v1, /device:TPU:1, one launch (start us, length us, event | category | flops | bytes accessed | tf_op | source)
XLA Modules:
  0.0 58.3 jit_solution(11362031684126185872)
XLA Ops:
  1.9 0.0 copy-start
  1.9 1.2 %copy-done = bf16[512,1024]{1,0:T(8,128)(2,1)S(1)} copy-done((bf16[512,1024]{1,0:T(8,128)(2,1)S(1)}, bf16[512,1024]{1,0:T(8,128)(2,1)}, u32[]{:S(2)}) %copy-start) | copy-done | bytes 1048600
  3.1 0.0 copy-start.1
  3.2 1.0 %copy-done.1 = bf16[1,256,1024]{2,1,0:T(8,128)(2,1)S(1)} copy-done((bf16[1,256,1024]{2,1,0:T(8,128)(2,1)S(1)}, bf16[1,256,1024]{2,1,0:T(8,128)(2,1)}, u32[]{:S(2)}) %copy-start.1) | copy-done | bytes 524312
  4.2 0.0 copy-start.2
  4.2 1.0 %copy-done.2 = bf16[1,256,1024]{2,1,0:T(8,128)(2,1)S(1)} copy-done((bf16[1,256,1024]{2,1,0:T(8,128)(2,1)S(1)}, bf16[1,256,1024]{2,1,0:T(8,128)(2,1)}, u32[]{:S(2)}) %copy-start.2) | copy-done | bytes 524312
  5.2 0.0 copy-start.3
  5.2 1.0 %copy-done.3 = bf16[1,256,1024]{2,1,0:T(8,128)(2,1)S(1)} copy-done((bf16[1,256,1024]{2,1,0:T(8,128)(2,1)S(1)}, bf16[1,256,1024]{2,1,0:T(8,128)(2,1)}, u32[]{:S(2)}) %copy-start.3) | copy-done | bytes 524312
  6.3 0.0 copy-start.4
  6.3 1.0 %copy-done.4 = bf16[1,256,1024]{2,1,0:T(8,128)(2,1)S(1)} copy-done((bf16[1,256,1024]{2,1,0:T(8,128)(2,1)S(1)}, bf16[1,256,1024]{2,1,0:T(8,128)(2,1)}, u32[]{:S(2)}) %copy-start.4) | copy-done | bytes 524312
  7.3 0.0 copy-start.5
  7.3 0.7 %copy-done.5 = bf16[1,4096]{1,0:T(2,128)(2,1)S(1)} copy-done((bf16[1,4096]{1,0:T(2,128)(2,1)S(1)}, bf16[1,4096]{1,0:T(2,128)(2,1)}, u32[]{:S(2)}) %copy-start.5) | copy-done | bytes 8216
  8.0 0.0 copy-start.6
  8.0 0.7 %copy-done.6 = bf16[1,1024]{1,0:T(2,128)(2,1)S(1)} copy-done((bf16[1,1024]{1,0:T(2,128)(2,1)S(1)}, bf16[1,1024]{1,0:T(2,128)(2,1)}, u32[]{:S(2)}) %copy-start.6) | copy-done | bytes 2072
  8.7 47.4 %shard_map.104 = (bf16[1,256,1024]{2,1,0:T(8,128)(2,1)S(1)}, f32[512,1024]{1,0:T(8,128)S(1)}) custom-call(bf16[1,256,1024]{2,1,0:T(8,128)(2,1)S(1)} %copy-done.1, bf16[1,256,1024]{2,1,0:T(8,128)(2,1)S(1)} %copy-done.2, bf16[1,256,1024]{2,1,0:T(8,128)(2,1)S(1)} %copy-done.3, bf16[1,256,1024]{2,1,0:T(8,128)(2,1)S(1)} %copy-done.4, ...), custom_call_target="tpu_custom_call" | custom-call | flops 2147483648 | bytes 16777216 | tf_op jit(solution)/shard_map/pallas_call | solution.py:389
  56.1 0.8 %copy.15 = bf16[1,256,1024]{2,1,0:T(8,128)(2,1)} copy(bf16[1,256,1024]{2,1,0:T(8,128)(2,1)S(1)} %get-tuple-element.4) | data formatting | bytes 1048576
  56.9 1.3 %copy.16 = f32[512,1024]{1,0:T(8,128)} copy(f32[512,1024]{1,0:T(8,128)S(1)} %get-tuple-element.5) | data formatting | bytes 4194304
Async XLA Ops:
  1.9 1.2 %copy-start = (bf16[512,1024]{1,0:T(8,128)(2,1)S(1)}, bf16[512,1024]{1,0:T(8,128)(2,1)}, u32[]{:S(2)}) copy-start(bf16[512,1024]{1,0:T(8,128)(2,1)} %w.1) | copy-start | bytes 3145732
  3.1 1.0 %copy-start.1 = (bf16[1,256,1024]{2,1,0:T(8,128)(2,1)S(1)}, bf16[1,256,1024]{2,1,0:T(8,128)(2,1)}, u32[]{:S(2)}) copy-start(bf16[1,256,1024]{2,1,0:T(8,128)(2,1)} %tok.1) | copy-start | bytes 1572868
  4.2 1.0 %copy-start.2 = (bf16[1,256,1024]{2,1,0:T(8,128)(2,1)S(1)}, bf16[1,256,1024]{2,1,0:T(8,128)(2,1)}, u32[]{:S(2)}) copy-start(bf16[1,256,1024]{2,1,0:T(8,128)(2,1)} %rec.1) | copy-start | bytes 1572868
  5.2 1.0 %copy-start.3 = (bf16[1,256,1024]{2,1,0:T(8,128)(2,1)S(1)}, bf16[1,256,1024]{2,1,0:T(8,128)(2,1)}, u32[]{:S(2)}) copy-start(bf16[1,256,1024]{2,1,0:T(8,128)(2,1)} %key.1) | copy-start | bytes 1572868
  6.3 1.0 %copy-start.4 = (bf16[1,256,1024]{2,1,0:T(8,128)(2,1)S(1)}, bf16[1,256,1024]{2,1,0:T(8,128)(2,1)}, u32[]{:S(2)}) copy-start(bf16[1,256,1024]{2,1,0:T(8,128)(2,1)} %dec.1) | copy-start | bytes 1572868
  7.3 0.7 %copy-start.5 = (bf16[1,4096]{1,0:T(2,128)(2,1)S(1)}, bf16[1,4096]{1,0:T(2,128)(2,1)}, u32[]{:S(2)}) copy-start(bf16[1,4096]{1,0:T(2,128)(2,1)} %nin.1) | copy-start | bytes 24580
  8.0 0.7 %copy-start.6 = (bf16[1,1024]{1,0:T(2,128)(2,1)S(1)}, bf16[1,1024]{1,0:T(2,128)(2,1)}, u32[]{:S(2)}) copy-start(bf16[1,1024]{1,0:T(2,128)(2,1)} %nout.1) | copy-start | bytes 6148

commit v2 on v1

--- a/solution.py
+++ b/solution.py
@@ -34,18 +34,24 @@
     pop,
     tp,
     tok,
-    rec,
-    key,
-    dec,
+    rec_hbm,
+    key_hbm,
+    dec_hbm,
     w,
-    nin,
-    nout,
+    nin_hbm,
+    nout_hbm,
     util,
     live,
     wkv,
     upd,
     tok_buf,
     wbuf,
+    rec,
+    key,
+    dec,
+    nin,
+    nout,
+    acc,
     s_low,
     s_high,
     proj,
@@ -103,16 +109,17 @@
 
     own_tok = pltpu.make_async_copy(tok.at[0], tok_buf.at[k], own_sem.at[0])
     own_w = pltpu.make_async_copy(w, wbuf.at[pl.ds(pl.multiple_of(p * rows, rows), rows)], own_sem.at[1])
+    loads = [
+        pltpu.make_async_copy(src, dst, own_sem.at[2 + i])
+        for i, (src, dst) in enumerate(
+            ((nin_hbm, nin), (nout_hbm, nout), (dec_hbm, dec), (rec_hbm, rec), (key_hbm, key))
+        )
+    ]
+    for copy in loads:
+        copy.start()
     own_tok.start()
     own_w.start()
 
-    scale = util[0] * (1.0 / math.sqrt(pop))
-    weighted = nin[...].astype(F32) * scale
-    out_factor = nout[...].astype(F32)
-    for dest in range(pop):
-        start = dest * rows // LANES * LANES
-        small_src[dest, :, 0:win] = weighted[:, start : start + win]
-        small_src[dest, :, win : win + width] = out_factor
     neighbours = jnp.where(k >= 1, 1, 0) + jnp.where(k <= tp - 2, 1, 0)
     pl.semaphore_wait(barrier, pop - 1 + neighbours)
 
@@ -197,17 +204,25 @@
     for i in range(WCUTS):
         send(own_piece(x_order[i]), piece(q, x_order[i]), x_send, x_recv, x_order[i], qx)
         send(own_piece(y_order[i]), piece(q, y_order[i]), y_send, y_recv, y_order[i], qy)
-        if i == 0:
-            for d in range(1, pop):
-                target = lax.rem(p + d, pop)
-                copy = remote(
-                    small_src.at[target], small_dst.at[p], small_send.at[d - 1], small_recv.at[d - 1], pop=target
-                )
-                copy.start()
-                sent.append(copy)
     for i in range(WCUTS):
         send(own_piece(i), piece(q, i), c_send, c_recv, i, qc)
+    loads[0].wait()
+    loads[1].wait()
+    scale = util[0] * (1.0 / math.sqrt(pop))
+    weighted = nin[...].astype(F32) * scale
+    out_factor = nout[...].astype(F32)
+    for dest in range(pop):
+        start = dest * rows // LANES * LANES
+        small_src[dest, :, 0:win] = weighted[:, start : start + win]
+        small_src[dest, :, win : win + width] = out_factor
+    for d in range(1, pop):
+        target = lax.rem(p + d, pop)
+        copy = remote(small_src.at[target], small_dst.at[p], small_send.at[d - 1], small_recv.at[d - 1], pop=target)
+        copy.start()
+        sent.append(copy)
     small_dst[p] = small_src[p]
+    for copy in loads[2:]:
+        copy.wait()
 
     def round_of(i):
         if i < WCUTS:
@@ -248,7 +263,14 @@
         return jnp.concatenate([jnp.broadcast_to(cum[a : a + 1], (count, LANES)) for a in at], 0)
 
     def heads_of(queries):
-        return jnp.concatenate([queries * first, queries * second], 0).astype(BF16)
+        high = queries.astype(BF16).astype(F32)
+        low = queries - high
+        terms = [jnp.concatenate([high * m, low * m], 1) for m in (first, second)]
+        return jnp.concatenate(terms, 0).astype(BF16)
+
+    def twice(keys):
+        keys = keys.astype(BF16)
+        return jnp.concatenate([keys, keys], 1)
 
     def scores_of(index):
         lanes = pl.ds(pl.multiple_of(index * LANES, LANES), LANES)
@@ -259,7 +281,7 @@
         decay = (dec[0, :, lanes].astype(F32) * mask).astype(BF16)
         cum = dot_nn(lower, decay)
         fade = jnp.exp(-jnp.abs(cum - cum[half - 1 : half]))
-        cross = dot_nt(heads_of(recept[half:] * fade[half:]), (keys[:half] * fade[:half]).astype(BF16))
+        cross = dot_nt(heads_of(recept[half:] * fade[half:]), twice(keys[:half] * fade[:half]))
         far = jnp.exp(-jnp.abs(cum - spread(cum, (63, 191), half)))
         near = jnp.exp(-jnp.abs(cum - spread(cum, (31, 95, 159, 223), 64)))
         inner = cum - spread(cum, tuple(range(15, length, span)), span)
@@ -268,9 +290,9 @@
         for h in range(2):
             part = slice(h * half, (h + 1) * half)
             r, kk = recept[part], keys[part]
-            far_s = dot_nt(heads_of(r * far[part]), (kk * far[part]).astype(BF16))
-            near_s = dot_nt(heads_of(r * near[part]), (kk * near[part]).astype(BF16))
-            diag_s = dot_nt(heads_of(r * grow[part]), (kk * shrink[part]).astype(BF16))
+            far_s = dot_nt(heads_of(r * far[part]), twice(kk * far[part]))
+            near_s = dot_nt(heads_of(r * near[part]), twice(kk * near[part]))
+            diag_s = dot_nt(heads_of(r * grow[part]), twice(kk * shrink[part]))
             for a in range(2):
                 sel = slice(a * half, (a + 1) * half)
                 out.append(
@@ -312,40 +334,126 @@
     offset = pl.multiple_of(lax.rem(p * rows, LANES) if rows < LANES else 0, 8)
     upd_copy = pltpu.make_async_copy(upd_buf.at[pl.ds(offset, rows)], upd, upd_sem)
 
+    tile = 2 * LANES
+    qxc, qyc, qdc = flip(qx, 1), flip(qy, 1), flip(qd, 1)
+    near_blocks = (q, qc, qx, qxc, qy, qyc)
+    last_blocks = (qd, qdc)
+    all_pieces = tuple(range(WCUTS))
+
+    def distance(index):
+        j = lax.div(index * block, width)
+        return jnp.maximum(j - k, k - j)
+
+    def is_far(index):
+        return distance(index) >= tp - 1
+
+    def multiply(index, pieces, begin, end):
+        j = lax.div(index * block, width)
+        base = lax.rem(index * block, width)
+        if pieces == all_pieces:
+            spans = [(0, block)]
+        else:
+            spans = [(c * cut, cut) for c in pieces]
+
+        @pl.loop(0, width // tile)
+        def _(n):
+            lanes = pl.ds(pl.multiple_of(n * tile, tile), tile)
+            left = [tok_buf[j, begin:end, pl.ds(pl.multiple_of(base + o, LANES), size)] for o, size in spans]
+            right = [wbuf[pl.ds(pl.multiple_of(index * block + o, LANES), size), lanes] for o, size in spans]
+            if len(spans) > 1:
+                left, right = [jnp.concatenate(left, 1)], [jnp.concatenate(right, 0)]
+            acc[begin:end, lanes] += dot_nn(left[0], right[0])
+
+    def project(j):
+        part = jnp.broadcast_to(nin[:, j * width : (j + 1) * width].astype(F32), (LANES, width)).astype(BF16)
+        proj[...] += dot_nt(tok_buf[j], part)
+
+    def arrived(index, b, pieces):
+        for c in pieces:
+            landed(index, c, c_recv, b * WCUTS + c)
+
+    acc[...] = jnp.zeros_like(acc)
+    proj[...] = jnp.zeros_like(proj)
     rounds = WCUTS + WCUTS // 2
-    bounds = [pairs * (i + 1) // rounds for i in range(rounds)]
+    bounds = [pairs * share // 8 for share in (3, 5, 7, 8, 8, 8)]
+    early = (x_order[0], y_order[0])
+    late = (x_order[1], y_order[1])
     for i in range(rounds):
         score_pairs(done, bounds[i])
         done = bounds[i]
         round_of(i)
-        if i == 1:
-            update_part()
-            upd_copy.start()
         step, c = divmod(i, TCUTS)
         if step <= tp - 2:
             take_tokens(step, c)
-
-    own_tok.wait()
-    for b, index in enumerate((qc, flip(qx, 1), flip(qy, 1), flip(qd, 1))):
-        for c in range(WCUTS):
-            landed(index, c, c_recv, b * WCUTS + c)
-    if group == 1:
-        own_w.wait()
-
-    total = jnp.zeros((length, LANES), F32)
+        if i == 2:
+            update_part()
+            upd_copy.start()
+        if i == 3:
+            own_tok.wait()
+            if group == 1:
+                own_w.wait()
+            for b, index in enumerate((qc, qxc, qyc)):
+                arrived(index, b, all_pieces)
+            for index in near_blocks:
+
+                @pl.when(jnp.logical_not(is_far(index)))
+                def _():
+                    multiply(index, all_pieces, 0, length)
+
+            for j in range(tp):
+
+                @pl.when(jnp.maximum(j - k, k - j) < tp - 1)
+                def _():
+                    project(j)
+
+        if i == 4:
+            arrived(qdc, 3, early)
+            for index in near_blocks:
+
+                @pl.when(is_far(index))
+                def _():
+                    multiply(index, all_pieces, 0, half)
+
+            for index in last_blocks:
+
+                @pl.when(is_far(index))
+                def _():
+                    multiply(index, early, 0, half)
+
+                @pl.when(jnp.logical_not(is_far(index)))
+                def _():
+                    multiply(index, early, 0, length)
+
+    for index in near_blocks:
+
+        @pl.when(is_far(index))
+        def _():
+            multiply(index, all_pieces, half, length)
+
     for j in range(tp):
-        part = jnp.broadcast_to(nin[:, j * width : (j + 1) * width].astype(F32), (LANES, width)).astype(BF16)
-        total = total + dot_nt(tok_buf[j], part)
-    proj[...] = total * (SIGMA / math.sqrt(full))
-
-    tile = 2 * LANES
+
+        @pl.when(jnp.maximum(j - k, k - j) >= tp - 1)
+        def _():
+            project(j)
+
+    arrived(qdc, 3, late)
+    for index in last_blocks:
+
+        @pl.when(is_far(index))
+        def _():
+            multiply(index, late, 0, half)
+            multiply(index, all_pieces, half, length)
+
+        @pl.when(jnp.logical_not(is_far(index)))
+        def _():
+            multiply(index, late, 0, length)
+
+    factor = proj[...] * (SIGMA / math.sqrt(full))
 
     @pl.loop(0, width // tile)
     def _(n):
         lanes = pl.ds(pl.multiple_of(n * tile, tile), tile)
-        base = jnp.concatenate([proj[...], proj[...]], 1) * nout[:, lanes].astype(F32)
-        for j in range(tp):
-            base = base + dot_nn(tok_buf[j], wbuf[j * width : (j + 1) * width, lanes])
+        base = acc[:, lanes] + jnp.concatenate([factor, factor], 1) * nout[:, lanes].astype(F32)
         values = base.astype(BF16)
         for b in range(2):
             pair = values[:, b * LANES : (b + 1) * LANES].astype(F32)
@@ -386,24 +494,31 @@
     whole = pl.BlockSpec(memory_space=pltpu.VMEM)
     scalar = pl.BlockSpec(memory_space=pltpu.SMEM)
     anywhere = pl.BlockSpec(memory_space=pl.ANY)
+    hbm = pl.BlockSpec(memory_space=pltpu.HBM)
     return pl.pallas_call(
         functools.partial(kernel, pop, tp),
         out_shape=(
             jax.ShapeDtypeStruct((1, length, width), BF16),
             jax.ShapeDtypeStruct((rows, width), F32),
         ),
-        in_specs=[anywhere, whole, whole, whole, anywhere, whole, whole, scalar, scalar],
+        in_specs=[hbm] * 7 + [scalar] * 2,
         out_specs=(whole, anywhere),
         scratch_shapes=[
             pltpu.VMEM((tp, length, width), BF16),
             pltpu.VMEM((full, width), BF16),
+            pltpu.VMEM((1, length, width), BF16),
+            pltpu.VMEM((1, length, width), BF16),
+            pltpu.VMEM((1, length, width), BF16),
+            pltpu.VMEM((1, full), BF16),
+            pltpu.VMEM((1, width), BF16),
+            pltpu.VMEM((length, width), F32),
             pltpu.VMEM((pairs, half, 2 * half), BF16),
             pltpu.VMEM((pairs, half, 4 * half), BF16),
             pltpu.VMEM((length, LANES), F32),
             pltpu.VMEM((pop, 1, win + width), F32),
             pltpu.VMEM((pop, 1, win + width), F32),
             pltpu.VMEM((win, width), F32),
-            dma((2,)),
+            dma((7,)),
             dma,
             dma((pop - 1,)),
             dma((pop - 1,)),

time: 58.7 us -> 60.3 us (1.027)
  Pallas kernels: 47.4 us -> 49 us
    pallas_call x1, Pallas kernels: 47.4 us -> 49 us  [body(): pl.pallas_call(functools.partial(kernel, pop, tp), out_shape=(jax.ShapeDt...]
where the time goes in v2:
time: 60.3 us; the launch traced here: 59.8 us
  Pallas kernels  49 us (81%)
  local copies, waits for them, and re-layouts  8.9 us (15%)
  between operations  1.95 us (3%)
    pallas_call x1, Pallas kernels, body(): pl.pallas_call(functools.partial(kernel, pop, tp), out_shape=(jax.ShapeDt...  49 us
    unnamed x16, local copies, waits for them, and re-layouts  8.9 us

profile of v2, /device:TPU:1, one launch (start us, length us, event | category | flops | bytes accessed | tf_op | source)
XLA Modules:
  0.0 59.8 jit_solution(1317686522599470635)
XLA Ops:
  1.9 0.0 copy-start
  1.9 1.2 %copy-done = bf16[512,1024]{1,0:T(8,128)(2,1)S(1)} copy-done((bf16[512,1024]{1,0:T(8,128)(2,1)S(1)}, bf16[512,1024]{1,0:T(8,128)(2,1)}, u32[]{:S(2)}) %copy-start) | copy-done | bytes 1048600
  3.1 0.0 copy-start.1
  3.2 1.0 %copy-done.1 = bf16[1,256,1024]{2,1,0:T(8,128)(2,1)S(1)} copy-done((bf16[1,256,1024]{2,1,0:T(8,128)(2,1)S(1)}, bf16[1,256,1024]{2,1,0:T(8,128)(2,1)}, u32[]{:S(2)}) %copy-start.1) | copy-done | bytes 524312
  4.2 0.0 copy-start.2
  4.2 1.0 %copy-done.2 = bf16[1,256,1024]{2,1,0:T(8,128)(2,1)S(1)} copy-done((bf16[1,256,1024]{2,1,0:T(8,128)(2,1)S(1)}, bf16[1,256,1024]{2,1,0:T(8,128)(2,1)}, u32[]{:S(2)}) %copy-start.2) | copy-done | bytes 524312
  5.2 0.0 copy-start.3
  5.2 1.0 %copy-done.3 = bf16[1,256,1024]{2,1,0:T(8,128)(2,1)S(1)} copy-done((bf16[1,256,1024]{2,1,0:T(8,128)(2,1)S(1)}, bf16[1,256,1024]{2,1,0:T(8,128)(2,1)}, u32[]{:S(2)}) %copy-start.3) | copy-done | bytes 524312
  6.3 0.0 copy-start.4
  6.3 1.0 %copy-done.4 = bf16[1,256,1024]{2,1,0:T(8,128)(2,1)S(1)} copy-done((bf16[1,256,1024]{2,1,0:T(8,128)(2,1)S(1)}, bf16[1,256,1024]{2,1,0:T(8,128)(2,1)}, u32[]{:S(2)}) %copy-start.4) | copy-done | bytes 524312
  7.3 0.0 copy-start.5
  7.3 0.7 %copy-done.5 = bf16[1,4096]{1,0:T(2,128)(2,1)S(1)} copy-done((bf16[1,4096]{1,0:T(2,128)(2,1)S(1)}, bf16[1,4096]{1,0:T(2,128)(2,1)}, u32[]{:S(2)}) %copy-start.5) | copy-done | bytes 8216
  8.0 0.0 copy-start.6
  8.0 0.7 %copy-done.6 = bf16[1,1024]{1,0:T(2,128)(2,1)S(1)} copy-done((bf16[1,1024]{1,0:T(2,128)(2,1)S(1)}, bf16[1,1024]{1,0:T(2,128)(2,1)}, u32[]{:S(2)}) %copy-start.6) | copy-done | bytes 2072
  8.7 49.0 %shard_map.104 = (bf16[1,256,1024]{2,1,0:T(8,128)(2,1)S(1)}, f32[512,1024]{1,0:T(8,128)S(1)}) custom-call(bf16[1,256,1024]{2,1,0:T(8,128)(2,1)S(1)} %copy-done.1, bf16[1,256,1024]{2,1,0:T(8,128)(2,1)S(1)} %copy-done.2, bf16[1,256,1024]{2,1,0:T(8,128)(2,1)S(1)} %copy-done.3, bf16[1,256,1024]{2,1,0:T(8,128)(2,1)S(1)} %copy-done.4, ...), custom_call_target="tpu_custom_call" | custom-call | flops 2147483648 | bytes 16777216 | tf_op jit(solution)/shard_map/pallas_call | solution.py:498
  57.7 0.8 %copy.15 = bf16[1,256,1024]{2,1,0:T(8,128)(2,1)} copy(bf16[1,256,1024]{2,1,0:T(8,128)(2,1)S(1)} %get-tuple-element.4) | data formatting | bytes 1048576
  58.5 1.3 %copy.16 = f32[512,1024]{1,0:T(8,128)} copy(f32[512,1024]{1,0:T(8,128)S(1)} %get-tuple-element.5) | data formatting | bytes 4194304
Async XLA Ops:
  1.9 1.2 %copy-start = (bf16[512,1024]{1,0:T(8,128)(2,1)S(1)}, bf16[512,1024]{1,0:T(8,128)(2,1)}, u32[]{:S(2)}) copy-start(bf16[512,1024]{1,0:T(8,128)(2,1)} %w.1) | copy-start | bytes 3145732
  3.1 1.0 %copy-start.1 = (bf16[1,256,1024]{2,1,0:T(8,128)(2,1)S(1)}, bf16[1,256,1024]{2,1,0:T(8,128)(2,1)}, u32[]{:S(2)}) copy-start(bf16[1,256,1024]{2,1,0:T(8,128)(2,1)} %tok.1) | copy-start | bytes 1572868
  4.2 1.0 %copy-start.2 = (bf16[1,256,1024]{2,1,0:T(8,128)(2,1)S(1)}, bf16[1,256,1024]{2,1,0:T(8,128)(2,1)}, u32[]{:S(2)}) copy-start(bf16[1,256,1024]{2,1,0:T(8,128)(2,1)} %rec_hbm.1) | copy-start | bytes 1572868
  5.2 1.0 %copy-start.3 = (bf16[1,256,1024]{2,1,0:T(8,128)(2,1)S(1)}, bf16[1,256,1024]{2,1,0:T(8,128)(2,1)}, u32[]{:S(2)}) copy-start(bf16[1,256,1024]{2,1,0:T(8,128)(2,1)} %key_hbm.1) | copy-start | bytes 1572868
  6.3 1.0 %copy-start.4 = (bf16[1,256,1024]{2,1,0:T(8,128)(2,1)S(1)}, bf16[1,256,1024]{2,1,0:T(8,128)(2,1)}, u32[]{:S(2)}) copy-start(bf16[1,256,1024]{2,1,0:T(8,128)(2,1)} %dec_hbm.1) | copy-start | bytes 1572868
  7.3 0.7 %copy-start.5 = (bf16[1,4096]{1,0:T(2,128)(2,1)S(1)}, bf16[1,4096]{1,0:T(2,128)(2,1)}, u32[]{:S(2)}) copy-start(bf16[1,4096]{1,0:T(2,128)(2,1)} %nin_hbm.1) | copy-start | bytes 24580
  8.0 0.7 %copy-start.6 = (bf16[1,1024]{1,0:T(2,128)(2,1)S(1)}, bf16[1,1024]{1,0:T(2,128)(2,1)}, u32[]{:S(2)}) copy-start(bf16[1,1024]{1,0:T(2,128)(2,1)} %nout_hbm.1) | copy-start | bytes 6148

commit v3 on v2

--- a/solution.py
+++ b/solution.py
@@ -263,14 +263,7 @@
         return jnp.concatenate([jnp.broadcast_to(cum[a : a + 1], (count, LANES)) for a in at], 0)
 
     def heads_of(queries):
-        high = queries.astype(BF16).astype(F32)
-        low = queries - high
-        terms = [jnp.concatenate([high * m, low * m], 1) for m in (first, second)]
-        return jnp.concatenate(terms, 0).astype(BF16)
-
-    def twice(keys):
-        keys = keys.astype(BF16)
-        return jnp.concatenate([keys, keys], 1)
+        return jnp.concatenate([queries * first, queries * second], 0).astype(BF16)
 
     def scores_of(index):
         lanes = pl.ds(pl.multiple_of(index * LANES, LANES), LANES)
@@ -281,7 +274,7 @@
         decay = (dec[0, :, lanes].astype(F32) * mask).astype(BF16)
         cum = dot_nn(lower, decay)
         fade = jnp.exp(-jnp.abs(cum - cum[half - 1 : half]))
-        cross = dot_nt(heads_of(recept[half:] * fade[half:]), twice(keys[:half] * fade[:half]))
+        cross = dot_nt(heads_of(recept[half:] * fade[half:]), (keys[:half] * fade[:half]).astype(BF16))
         far = jnp.exp(-jnp.abs(cum - spread(cum, (63, 191), half)))
         near = jnp.exp(-jnp.abs(cum - spread(cum, (31, 95, 159, 223), 64)))
         inner = cum - spread(cum, tuple(range(15, length, span)), span)
@@ -290,9 +283,9 @@
         for h in range(2):
             part = slice(h * half, (h + 1) * half)
             r, kk = recept[part], keys[part]
-            far_s = dot_nt(heads_of(r * far[part]), twice(kk * far[part]))
-            near_s = dot_nt(heads_of(r * near[part]), twice(kk * near[part]))
-            diag_s = dot_nt(heads_of(r * grow[part]), twice(kk * shrink[part]))
+            far_s = dot_nt(heads_of(r * far[part]), (kk * far[part]).astype(BF16))
+            near_s = dot_nt(heads_of(r * near[part]), (kk * near[part]).astype(BF16))
+            diag_s = dot_nt(heads_of(r * grow[part]), (kk * shrink[part]).astype(BF16))
             for a in range(2):
                 sel = slice(a * half, (a + 1) * half)
                 out.append(
@@ -312,9 +305,10 @@
     done = 0
 
     def score_pairs(begin, end):
-        @pl.loop(begin, end)
+        @pl.loop(begin // 2, end // 2)
         def _(index):
-            scores_of(index)
+            scores_of(index * 2)
+            scores_of(index * 2 + 1)
 
     def update_part():
         for d in range(1, pop):
@@ -375,7 +369,7 @@
     acc[...] = jnp.zeros_like(acc)
     proj[...] = jnp.zeros_like(proj)
     rounds = WCUTS + WCUTS // 2
-    bounds = [pairs * share // 8 for share in (3, 5, 7, 8, 8, 8)]
+    bounds = [pairs * share // 8 for share in (2, 4, 6, 6, 8, 8)]
     early = (x_order[0], y_order[0])
     late = (x_order[1], y_order[1])
     for i in range(rounds):
@@ -385,10 +379,9 @@
         step, c = divmod(i, TCUTS)
         if step <= tp - 2:
             take_tokens(step, c)
-        if i == 2:
+        if i == 3:
             update_part()
             upd_copy.start()
-        if i == 3:
             own_tok.wait()
             if group == 1:
                 own_w.wait()
@@ -536,7 +529,7 @@
             dma((tp - 1, TCUTS)),
         ],
         compiler_params=pltpu.CompilerParams(
-            collective_id=0, has_side_effects=True, vmem_limit_bytes=48 * 1024 * 1024
+            collective_id=0, has_side_effects=True, vmem_limit_bytes=63 * 1024 * 1024
         ),
         cost_estimate=pl.CostEstimate(
             flops=2 * length * full * width, bytes_accessed=16 * 1024 * 1024, transcendentals=5 * length * width

time: 60.3 us -> 56 us (0.929)
  local copies, waits for them, and re-layouts: 8.9 us -> 5.03 us
    unnamed x16 -> x2, local copies, waits for them, and re-layouts: 8.9 us -> 5.03 us
where the time goes in v3:
time: 56 us; the launch traced here: 55.5 us
  Pallas kernels  48.5 us (87%)
  local copies, waits for them, and re-layouts  5.03 us (9%)
  between operations  1.93 us (3%)
    pallas_call x1, Pallas kernels, body(): pl.pallas_call(functools.partial(kernel, pop, tp), out_shape=(jax.ShapeDt...  48.5 us
    unnamed x2, local copies, waits for them, and re-layouts  5.03 us

profile of v3, /device:TPU:1, one launch (start us, length us, event | category | flops | bytes accessed | tf_op | source)
XLA Modules:
  0.0 55.5 jit_solution(14568775203904666132)
XLA Ops:
  1.9 48.5 %shard_map.104 = (bf16[1,256,1024]{2,1,0:T(8,128)(2,1)}, f32[512,1024]{1,0:T(8,128)}) custom-call(bf16[1,256,1024]{2,1,0:T(8,128)(2,1)} %tok.1, bf16[1,256,1024]{2,1,0:T(8,128)(2,1)} %rec_hbm.1, bf16[1,256,1024]{2,1,0:T(8,128)(2,1)} %key_hbm.1, bf16[1,256,1024]{2,1,0:T(8,128)(2,1)} %dec_hbm.1, bf16[512,1024]{1,0:T(8,128)(2,1)} %w.1, ...), custom_call_target="tpu_custom_call" | custom-call | flops 2147483648 | bytes 16777216 | tf_op jit(solution)/shard_map/pallas_call | solution.py:491
  50.5 1.9 %copy.15 = bf16[1,256,1024]{2,1,0:T(8,128)(2,1)} copy(bf16[1,256,1024]{2,1,0:T(8,128)(2,1)} %get-tuple-element.4) | data formatting | bytes 1048576
  52.4 3.2 %copy.16 = f32[512,1024]{1,0:T(8,128)} copy(f32[512,1024]{1,0:T(8,128)} %get-tuple-element.5) | data formatting | bytes 4194304

commit v4 on v3

--- a/solution.py
+++ b/solution.py
@@ -42,8 +42,9 @@
     nout_hbm,
     util,
     live,
-    wkv,
-    upd,
+    wkv_hbm,
+    left_out,
+    right_out,
     tok_buf,
     wbuf,
     rec,
@@ -57,9 +58,10 @@
     proj,
     small_src,
     small_dst,
-    upd_buf,
+    factor_buf,
+    wkv,
     own_sem,
-    upd_sem,
+    wkv_sem,
     small_send,
     small_recv,
     group_send,
@@ -82,7 +84,7 @@
     block = rows * group
     cut = block // WCUTS
     tcut = length // TCUTS
-    win = upd_buf.shape[0]
+    win = factor_buf.shape[0]
     half = length // 2
 
     p = lax.axis_index("pop")
@@ -183,8 +185,7 @@
         here = piece(index, c)
         remote(here, here, x_send.at[0], recvs.at[slot], pop=p).wait_recv()
 
-    for c in range(TCUTS):
-        start_tokens(0, c)
+    start_tokens(0, 0)
 
     if group > 1:
         mine = wbuf.at[pl.ds(pl.multiple_of(p * rows, rows), rows)]
@@ -201,11 +202,12 @@
 
     x_order = list(range(WCUTS))
     y_order = x_order[WCUTS // 2 :] + x_order[: WCUTS // 2]
-    for i in range(WCUTS):
+    def send_own(i):
         send(own_piece(x_order[i]), piece(q, x_order[i]), x_send, x_recv, x_order[i], qx)
         send(own_piece(y_order[i]), piece(q, y_order[i]), y_send, y_recv, y_order[i], qy)
-    for i in range(WCUTS):
-        send(own_piece(i), piece(q, i), c_send, c_recv, i, qc)
+
+    send_own(0)
+    send_own(1)
     loads[0].wait()
     loads[1].wait()
     scale = util[0] * (1.0 / math.sqrt(pop))
@@ -302,7 +304,6 @@
         s_high[index, :, 3 * half : 4 * half] = out[3]
 
     pairs = width // LANES
-    done = 0
 
     def score_pairs(begin, end):
         @pl.loop(begin // 2, end // 2)
@@ -319,14 +320,11 @@
         high = factor.astype(BF16).astype(F32)
         mid = (factor - high).astype(BF16).astype(F32)
         low = factor - high - mid
-        left = jnp.concatenate([high, mid, low], 0).T.astype(BF16)
-        for n in range(0, width, 256):
-            right = jnp.concatenate([small_dst[m, :, win + n : win + n + 256] for m in range(pop)], 0)
-            right = jnp.concatenate([right, right, right], 0).astype(BF16)
-            upd_buf[:, n : n + 256] = dot_nn(left, right)
-
-    offset = pl.multiple_of(lax.rem(p * rows, LANES) if rows < LANES else 0, 8)
-    upd_copy = pltpu.make_async_copy(upd_buf.at[pl.ds(offset, rows)], upd, upd_sem)
+        factor_buf[...] = jnp.concatenate([high, mid, low], 0).T
+        offset = pl.multiple_of(lax.rem(p * rows, LANES) if rows < LANES else 0, 8)
+        left_out[...] = factor_buf[pl.ds(offset, rows), :].astype(BF16)
+        right = jnp.concatenate([small_dst[m, :, win : win + width] for m in range(pop)], 0)
+        right_out[...] = jnp.concatenate([right, right, right], 0).astype(BF16)
 
     tile = 2 * LANES
     qxc, qyc, qdc = flip(qx, 1), flip(qy, 1), flip(qd, 1)
@@ -368,55 +366,65 @@
 
     acc[...] = jnp.zeros_like(acc)
     proj[...] = jnp.zeros_like(proj)
-    rounds = WCUTS + WCUTS // 2
-    bounds = [pairs * share // 8 for share in (2, 4, 6, 6, 8, 8)]
     early = (x_order[0], y_order[0])
     late = (x_order[1], y_order[1])
-    for i in range(rounds):
-        score_pairs(done, bounds[i])
-        done = bounds[i]
-        round_of(i)
-        step, c = divmod(i, TCUTS)
-        if step <= tp - 2:
-            take_tokens(step, c)
-        if i == 3:
-            update_part()
-            upd_copy.start()
-            own_tok.wait()
-            if group == 1:
-                own_w.wait()
-            for b, index in enumerate((qc, qxc, qyc)):
-                arrived(index, b, all_pieces)
-            for index in near_blocks:
-
-                @pl.when(jnp.logical_not(is_far(index)))
-                def _():
-                    multiply(index, all_pieces, 0, length)
-
-            for j in range(tp):
-
-                @pl.when(jnp.maximum(j - k, k - j) < tp - 1)
-                def _():
-                    project(j)
-
-        if i == 4:
-            arrived(qdc, 3, early)
-            for index in near_blocks:
-
-                @pl.when(is_far(index))
-                def _():
-                    multiply(index, all_pieces, 0, half)
-
-            for index in last_blocks:
-
-                @pl.when(is_far(index))
-                def _():
-                    multiply(index, early, 0, half)
-
-                @pl.when(jnp.logical_not(is_far(index)))
-                def _():
-                    multiply(index, early, 0, length)
-
+    share = pairs // 4
+    score_pairs(0, share)
+    start_tokens(0, 1)
+    send_own(2)
+    for i in range(WCUTS):
+        send(own_piece(i), piece(q, i), c_send, c_recv, i, qc)
+    take_tokens(0, 0)
+    round_of(0)
+    round_of(1)
+    send_own(3)
+    take_tokens(0, 1)
+    score_pairs(share, 3 * share)
+    take_tokens(1, 0)
+    take_tokens(1, 1)
+    round_of(2)
+    round_of(3)
+    score_pairs(3 * share, pairs)
+    update_part()
+
+    own_tok.wait()
+    if group == 1:
+        own_w.wait()
+    for b, index in enumerate((qc, qxc, qyc)):
+        arrived(index, b, all_pieces)
+    for index in near_blocks:
+
+        @pl.when(jnp.logical_not(is_far(index)))
+        def _():
+            multiply(index, all_pieces, 0, length)
+
+    for j in range(tp):
+
+        @pl.when(jnp.maximum(j - k, k - j) < tp - 1)
+        def _():
+            project(j)
+
+    round_of(4)
+    take_tokens(2, 0)
+    arrived(qdc, 3, early)
+    for index in near_blocks:
+
+        @pl.when(is_far(index))
+        def _():
+            multiply(index, all_pieces, 0, half)
+
+    for index in last_blocks:
+
+        @pl.when(is_far(index))
+        def _():
+            multiply(index, early, 0, half)
+
+        @pl.when(jnp.logical_not(is_far(index)))
+        def _():
+            multiply(index, early, 0, length)
+
+    round_of(5)
+    take_tokens(2, 1)
     for index in near_blocks:
 
         @pl.when(is_far(index))
@@ -459,6 +467,8 @@
             wkv[0, 0:half, here] = dot_nn(s_low[index], low_v).astype(BF16)
             wkv[0, half:length, here] = dot_nn(s_high[index], high_v).astype(BF16)
 
+    wkv_copy = pltpu.make_async_copy(wkv, wkv_hbm, wkv_sem)
+    wkv_copy.start()
     for copy in sent:
         copy.wait_send()
     for s in range(tp - 1):
@@ -472,7 +482,24 @@
             def _():
                 up(s, c).wait_send()
 
-    upd_copy.wait()
+    wkv_copy.wait()
+
+
+def finish(wkv_in, left, right, wkv, upd, upd_buf, sems, wkv_sem):
+    copy = pltpu.make_async_copy(wkv_in, wkv, wkv_sem)
+    copy.start()
+    count = sems.shape[0]
+    size = upd_buf.shape[0] // count
+    copies = []
+    for i in range(count):
+        here = slice(i * size, (i + 1) * size)
+        upd_buf[here, :] = dot_nn(left[here, :], right[...])
+        out = pltpu.make_async_copy(upd_buf.at[pl.ds(i * size, size)], upd.at[pl.ds(i * size, size)], sems.at[i])
+        out.start()
+        copies.append(out)
+    for out in copies:
+        out.wait()
+    copy.wait()
 
 
 def body(pop, tp, tokens, receptance, keys, log_decay, value_weight, noise_in, noise_out, utilities, live_length):
@@ -488,14 +515,15 @@
     scalar = pl.BlockSpec(memory_space=pltpu.SMEM)
     anywhere = pl.BlockSpec(memory_space=pl.ANY)
     hbm = pl.BlockSpec(memory_space=pltpu.HBM)
-    return pl.pallas_call(
+    wkv, left, right = pl.pallas_call(
         functools.partial(kernel, pop, tp),
         out_shape=(
             jax.ShapeDtypeStruct((1, length, width), BF16),
-            jax.ShapeDtypeStruct((rows, width), F32),
+            jax.ShapeDtypeStruct((rows, 3 * pop), BF16),
+            jax.ShapeDtypeStruct((3 * pop, width), BF16),
         ),
         in_specs=[hbm] * 7 + [scalar] * 2,
-        out_specs=(whole, anywhere),
+        out_specs=(anywhere, whole, whole),
         scratch_shapes=[
             pltpu.VMEM((tp, length, width), BF16),
             pltpu.VMEM((full, width), BF16),
@@ -510,7 +538,8 @@
             pltpu.VMEM((length, LANES), F32),
             pltpu.VMEM((pop, 1, win + width), F32),
             pltpu.VMEM((pop, 1, win + width), F32),
-            pltpu.VMEM((win, width), F32),
+            pltpu.VMEM((win, 3 * pop), F32),
+            pltpu.VMEM((1, length, width), BF16),
             dma((7,)),
             dma,
             dma((pop - 1,)),
@@ -535,6 +564,18 @@
             flops=2 * length * full * width, bytes_accessed=16 * 1024 * 1024, transcendentals=5 * length * width
         ),
     )(tokens, receptance, keys, log_decay, value_weight, noise_in, noise_out, utilities, live_length)
+    tiles = max(rows // LANES, 1)
+    return pl.pallas_call(
+        finish,
+        out_shape=(
+            jax.ShapeDtypeStruct((1, length, width), BF16),
+            jax.ShapeDtypeStruct((rows, width), F32),
+        ),
+        in_specs=[anywhere, whole, whole],
+        out_specs=(anywhere, anywhere),
+        scratch_shapes=[pltpu.VMEM((rows, width), F32), dma((tiles,)), dma],
+        compiler_params=pltpu.CompilerParams(vmem_limit_bytes=63 * 1024 * 1024),
+    )(wkv, left, right)
 
 
 def solution(mesh):

time: 56 us -> 79.4 us (1.42)
  Pallas kernels: 48.5 us -> 77.4 us
  local copies, waits for them, and re-layouts: 5.03 us -> 0 us
    pallas_call x0 -> x1, Pallas kernels: none -> 17.9 us  [body(): pl.pallas_call(finish, out_shape=(jax.ShapeDtypeStruct((1, length, width)...]
    pallas_call x1, Pallas kernels: 48.5 us -> 59.4 us  [body(): pl.pallas_call(functools.partial(kernel, pop, tp), out_shape=(jax.ShapeDt...]
    unnamed x2 -> x0, local copies, waits for them, and re-layouts: 5.03 us -> none
where the time goes in v4:
time: 79.4 us; the launch traced here: 79.3 us
  Pallas kernels  77.4 us (97%)
  between operations  1.93 us (2%)
    pallas_call x1, Pallas kernels, body(): pl.pallas_call(functools.partial(kernel, pop, tp), out_shape=(jax.ShapeDt...  59.4 us
    pallas_call x1, Pallas kernels, body(): pl.pallas_call(finish, out_shape=(jax.ShapeDtypeStruct((1, length, width)...  17.9 us

profile of v4, /device:TPU:1, one launch (start us, length us, event | category | flops | bytes accessed | tf_op | source)
XLA Modules:
  0.0 79.3 jit_solution(14870298215229300374)
XLA Ops:
  1.9 59.4 %shard_map.104 = (bf16[1,256,1024]{2,1,0:T(8,128)(2,1)}, bf16[512,24]{1,0:T(8,128)(2,1)}, bf16[24,1024]{1,0:T(8,128)(2,1)}) custom-call(bf16[1,256,1024]{2,1,0:T(8,128)(2,1)} %tok.1, bf16[1,256,1024]{2,1,0:T(8,128)(2,1)} %rec_hbm.1, bf16[1,256,1024]{2,1,0:T(8,128)(2,1)} %key_hbm.1, bf16[1,256,1024]{2,1,0:T(8,128)(2,1)} %dec_hbm.1, bf16[512,1024]{1,0:T(8,128)(2,1)} %w.1, ...), custom_call_target="tpu_custom_call" | custom-call | flops 2147483648 | bytes 16777216 | tf_op jit(solution)/shard_map/pallas_call | solution.py:518
  61.3 17.9 %shard_map.105 = (bf16[1,256,1024]{2,1,0:T(8,128)(2,1)}, f32[512,1024]{1,0:T(8,128)}) custom-call(bf16[1,256,1024]{2,1,0:T(8,128)(2,1)} %get-tuple-element.5.wkv_in, bf16[512,24]{1,0:T(8,128)(2,1)} %get-tuple-element.6.left, bf16[24,1024]{1,0:T(8,128)(2,1)} %get-tuple-element.7.right), custom_call_target="tpu_custom_call" | custom-call | tf_op jit(solution)/shard_map/pallas_call | solution.py:568

commit v5 on v4

--- a/solution.py
+++ b/solution.py
@@ -245,71 +245,71 @@
             send(piece(qd, cy), piece(qd, cy), c_send, c_recv, 3 * WCUTS + cy, qc)
 
     live_count = live[0]
+    quarter = length // 4
+    wide = 2 * LANES
     lane = lax.broadcasted_iota(jnp.int32, (half, LANES), 1)
-    first = (lane < HEAD).astype(F32)
-    second = 1.0 - first
-    row = lax.broadcasted_iota(jnp.int32, (half, LANES), 0)
-    masks = []
-    span = 32
+    first = (lane < HEAD).astype(BF16)
+    second = (lane >= HEAD).astype(BF16)
+    row = lax.broadcasted_iota(jnp.int32, (half, half), 0)
     col = lax.broadcasted_iota(jnp.int32, (half, half), 1)
-    prow = lax.broadcasted_iota(jnp.int32, (half, half), 0)
-    row_block, col_block = lax.div(prow, span), lax.div(col, span)
-    diag_mask = (row_block == col_block) & (col <= prow)
-    near_mask = (lax.rem(row_block, 2) == 1) & (col_block == row_block - 1)
-    far_mask = (row_block >= 2) & (col_block < 2)
+    diag_mask = (col <= row) & ((row < quarter) | (col >= quarter))
+    far_mask = lax.broadcasted_iota(jnp.int32, (quarter, half), 1) < quarter
     lower = (
         lax.broadcasted_iota(jnp.int32, (length, length), 0) >= lax.broadcasted_iota(jnp.int32, (length, length), 1)
     ).astype(BF16)
 
     def spread(cum, at, count):
-        return jnp.concatenate([jnp.broadcast_to(cum[a : a + 1], (count, LANES)) for a in at], 0)
+        return jnp.concatenate([jnp.broadcast_to(cum[a : a + 1], (count, cum.shape[1])) for a in at], 0)
 
     def heads_of(queries):
-        return jnp.concatenate([queries * first, queries * second], 0).astype(BF16)
-
-    def scores_of(index):
-        lanes = pl.ds(pl.multiple_of(index * LANES, LANES), LANES)
-        t = lax.broadcasted_iota(jnp.int32, (length, LANES), 0)
+        count = queries.shape[0]
+        return jnp.concatenate([queries * first[:count], queries * second[:count]], 0)
+
+    def scores_of(step):
+        lanes = pl.ds(pl.multiple_of(step * wide, wide), wide)
+        t = lax.broadcasted_iota(jnp.int32, (length, wide), 0)
         mask = (t < live_count).astype(F32)
         recept = rec[0, :, lanes].astype(F32) * mask
         keys = key[0, :, lanes].astype(F32) * mask
-        decay = (dec[0, :, lanes].astype(F32) * mask).astype(BF16)
-        cum = dot_nn(lower, decay)
+        cum = dot_nn(lower, dec[0, :, lanes] * mask.astype(BF16))
         fade = jnp.exp(-jnp.abs(cum - cum[half - 1 : half]))
-        cross = dot_nt(heads_of(recept[half:] * fade[half:]), (keys[:half] * fade[:half]).astype(BF16))
-        far = jnp.exp(-jnp.abs(cum - spread(cum, (63, 191), half)))
-        near = jnp.exp(-jnp.abs(cum - spread(cum, (31, 95, 159, 223), 64)))
-        inner = cum - spread(cum, tuple(range(15, length, span)), span)
-        grow, shrink = jnp.exp(inner), jnp.exp(-inner)
-        out = []
-        for h in range(2):
-            part = slice(h * half, (h + 1) * half)
-            r, kk = recept[part], keys[part]
-            far_s = dot_nt(heads_of(r * far[part]), (kk * far[part]).astype(BF16))
-            near_s = dot_nt(heads_of(r * near[part]), (kk * near[part]).astype(BF16))
-            diag_s = dot_nt(heads_of(r * grow[part]), (kk * shrink[part]).astype(BF16))
-            for a in range(2):
-                sel = slice(a * half, (a + 1) * half)
-                out.append(
-                    jnp.where(
-                        diag_mask, diag_s[sel], jnp.where(near_mask, near_s[sel], jnp.where(far_mask, far_s[sel], 0.0))
-                    ).astype(BF16)
+        q_cross = (recept[half:] * fade[half:]).astype(BF16)
+        k_cross = (keys[:half] * fade[:half]).astype(BF16)
+        far = jnp.exp(-jnp.abs(cum - spread(cum, (quarter - 1, half + quarter - 1), half)))
+        q_far = (recept * far).astype(BF16)
+        k_far = (keys * far).astype(BF16)
+        inner = cum - spread(cum, tuple(range(quarter // 2 - 1, length, quarter)), quarter)
+        q_diag = (recept * jnp.exp(inner)).astype(BF16)
+        k_diag = (keys * jnp.exp(-inner)).astype(BF16)
+        for b in range(wide // LANES):
+            index = step * (wide // LANES) + b
+            part = slice(b * LANES, (b + 1) * LANES)
+            cross = dot_nt(heads_of(q_cross[:, part]), k_cross[:, part]).astype(BF16)
+            s_high[index, :, 0:half] = cross[:half]
+            s_high[index, :, 2 * half : 3 * half] = cross[half:]
+            for h in range(2):
+                begin = h * half
+                diag_s = dot_nt(heads_of(q_diag[begin : begin + half, part]), k_diag[begin : begin + half, part])
+                far_s = dot_nt(
+                    heads_of(q_far[begin + quarter : begin + half, part]), k_far[begin : begin + half, part]
                 )
-        cross = cross.astype(BF16)
-        s_low[index, :, 0:half] = out[0]
-        s_low[index, :, half : 2 * half] = out[1]
-        s_high[index, :, 0:half] = cross[:half]
-        s_high[index, :, half : 2 * half] = out[2]
-        s_high[index, :, 2 * half : 3 * half] = cross[half:]
-        s_high[index, :, 3 * half : 4 * half] = out[3]
+                for a in range(2):
+                    own = jnp.where(diag_mask, diag_s[a * half : (a + 1) * half], 0.0)
+                    low = jnp.where(far_mask, far_s[a * quarter : (a + 1) * quarter], own[quarter:])
+                    if h == 0:
+                        s_low[index, 0:quarter, a * half : (a + 1) * half] = own[:quarter].astype(BF16)
+                        s_low[index, quarter:half, a * half : (a + 1) * half] = low.astype(BF16)
+                    else:
+                        at = (2 * a + 1) * half
+                        s_high[index, 0:quarter, at : at + half] = own[:quarter].astype(BF16)
+                        s_high[index, quarter:half, at : at + half] = low.astype(BF16)
 
     pairs = width // LANES
 
-    def score_pairs(begin, end):
-        @pl.loop(begin // 2, end // 2)
-        def _(index):
-            scores_of(index * 2)
-            scores_of(index * 2 + 1)
+    def score_steps(begin, end):
+        @pl.loop(begin, end)
+        def _(step):
+            scores_of(step)
 
     def update_part():
         for d in range(1, pop):
@@ -368,23 +368,24 @@
     proj[...] = jnp.zeros_like(proj)
     early = (x_order[0], y_order[0])
     late = (x_order[1], y_order[1])
-    share = pairs // 4
-    score_pairs(0, share)
+    steps = width // wide
+    share = steps // 4
     start_tokens(0, 1)
-    send_own(2)
     for i in range(WCUTS):
         send(own_piece(i), piece(q, i), c_send, c_recv, i, qc)
+    score_steps(0, share)
+    send_own(2)
+    send_own(3)
+    score_steps(share, 2 * share)
     take_tokens(0, 0)
+    take_tokens(0, 1)
     round_of(0)
     round_of(1)
-    send_own(3)
-    take_tokens(0, 1)
-    score_pairs(share, 3 * share)
+    score_steps(2 * share, steps)
     take_tokens(1, 0)
     take_tokens(1, 1)
     round_of(2)
     round_of(3)
-    score_pairs(3 * share, pairs)
     update_part()
 
     own_tok.wait()
@@ -457,9 +458,9 @@
         base = acc[:, lanes] + jnp.concatenate([factor, factor], 1) * nout[:, lanes].astype(F32)
         values = base.astype(BF16)
         for b in range(2):
-            pair = values[:, b * LANES : (b + 1) * LANES].astype(F32)
-            head_a = jnp.concatenate([pair[:half] * first, pair[half:] * first], 0).astype(BF16)
-            head_b = jnp.concatenate([pair[:half] * second, pair[half:] * second], 0).astype(BF16)
+            pair = values[:, b * LANES : (b + 1) * LANES]
+            head_a = jnp.concatenate([pair[:half] * first, pair[half:] * first], 0)
+            head_b = jnp.concatenate([pair[:half] * second, pair[half:] * second], 0)
             index = n * 2 + b
             low_v = jnp.concatenate([head_a[:half], head_b[:half]], 0)
             high_v = jnp.concatenate([head_a, head_b], 0)
@@ -485,9 +486,9 @@
     wkv_copy.wait()
 
 
-def finish(wkv_in, left, right, wkv, upd, upd_buf, sems, wkv_sem):
-    copy = pltpu.make_async_copy(wkv_in, wkv, wkv_sem)
-    copy.start()
+def finish(wkv_in, left, right, wkv, upd, upd_buf, wkv_buf, sems, wkv_sem):
+    fetch = pltpu.make_async_copy(wkv_in, wkv_buf, wkv_sem.at[0])
+    fetch.start()
     count = sems.shape[0]
     size = upd_buf.shape[0] // count
     copies = []
@@ -497,9 +498,13 @@
         out = pltpu.make_async_copy(upd_buf.at[pl.ds(i * size, size)], upd.at[pl.ds(i * size, size)], sems.at[i])
         out.start()
         copies.append(out)
+        if i == 0:
+            fetch.wait()
+            out = pltpu.make_async_copy(wkv_buf, wkv, wkv_sem.at[1])
+            out.start()
+            copies.append(out)
     for out in copies:
         out.wait()
-    copy.wait()
 
 
 def body(pop, tp, tokens, receptance, keys, log_decay, value_weight, noise_in, noise_out, utilities, live_length):
@@ -513,7 +518,6 @@
     dma = pltpu.SemaphoreType.DMA
     whole = pl.BlockSpec(memory_space=pltpu.VMEM)
     scalar = pl.BlockSpec(memory_space=pltpu.SMEM)
-    anywhere = pl.BlockSpec(memory_space=pl.ANY)
     hbm = pl.BlockSpec(memory_space=pltpu.HBM)
     wkv, left, right = pl.pallas_call(
         functools.partial(kernel, pop, tp),
@@ -523,7 +527,7 @@
             jax.ShapeDtypeStruct((3 * pop, width), BF16),
         ),
         in_specs=[hbm] * 7 + [scalar] * 2,
-        out_specs=(anywhere, whole, whole),
+        out_specs=(hbm, whole, whole),
         scratch_shapes=[
             pltpu.VMEM((tp, length, width), BF16),
             pltpu.VMEM((full, width), BF16),
@@ -571,9 +575,9 @@
             jax.ShapeDtypeStruct((1, length, width), BF16),
             jax.ShapeDtypeStruct((rows, width), F32),
         ),
-        in_specs=[anywhere, whole, whole],
-        out_specs=(anywhere, anywhere),
-        scratch_shapes=[pltpu.VMEM((rows, width), F32), dma((tiles,)), dma],
+        in_specs=[hbm, whole, whole],
+        out_specs=(hbm, hbm),
+        scratch_shapes=[pltpu.VMEM((rows, width), F32), pltpu.VMEM((1, length, width), BF16), dma((tiles,)), dma((2,))],
         compiler_params=pltpu.CompilerParams(vmem_limit_bytes=63 * 1024 * 1024),
     )(wkv, left, right)
 

time: 79.4 us -> 55.3 us (0.70)
  Pallas kernels: 77.4 us -> 53.2 us
    pallas_call x1, Pallas kernels: 17.9 us -> 3.34 us  [body(): pl.pallas_call(finish, out_shape=(jax.ShapeDtypeStruct((1, length, width)...]
    pallas_call x1, Pallas kernels: 59.4 us -> 49.8 us  [body(): pl.pallas_call(functools.partial(kernel, pop, tp), out_shape=(jax.ShapeDt...]
where the time goes in v5:
time: 55.3 us; the launch traced here: 55.1 us
  Pallas kernels  53.2 us (96%)
  between operations  1.93 us (3%)
    pallas_call x1, Pallas kernels, body(): pl.pallas_call(functools.partial(kernel, pop, tp), out_shape=(jax.ShapeDt...  49.8 us
    pallas_call x1, Pallas kernels, body(): pl.pallas_call(finish, out_shape=(jax.ShapeDtypeStruct((1, length, width)...  3.34 us

profile of v5, /device:TPU:1, one launch (start us, length us, event | category | flops | bytes accessed | tf_op | source)
XLA Modules:
  0.0 55.1 jit_solution(4312274658328553036)
XLA Ops:
  1.9 49.8 %shard_map.104 = (bf16[1,256,1024]{2,1,0:T(8,128)(2,1)}, bf16[512,24]{1,0:T(8,128)(2,1)}, bf16[24,1024]{1,0:T(8,128)(2,1)}) custom-call(bf16[1,256,1024]{2,1,0:T(8,128)(2,1)} %tok.1, bf16[1,256,1024]{2,1,0:T(8,128)(2,1)} %rec_hbm.1, bf16[1,256,1024]{2,1,0:T(8,128)(2,1)} %key_hbm.1, bf16[1,256,1024]{2,1,0:T(8,128)(2,1)} %dec_hbm.1, bf16[512,1024]{1,0:T(8,128)(2,1)} %w.1, ...), custom_call_target="tpu_custom_call" | custom-call | flops 2147483648 | bytes 16777216 | tf_op jit(solution)/shard_map/pallas_call | solution.py:522
  51.8 3.3 %shard_map.105 = (bf16[1,256,1024]{2,1,0:T(8,128)(2,1)}, f32[512,1024]{1,0:T(8,128)}) custom-call(bf16[1,256,1024]{2,1,0:T(8,128)(2,1)} %get-tuple-element.5.wkv_in, bf16[512,24]{1,0:T(8,128)(2,1)} %get-tuple-element.6.left, bf16[24,1024]{1,0:T(8,128)(2,1)} %get-tuple-element.7.right), custom_call_target="tpu_custom_call" | custom-call | tf_op jit(solution)/shard_map/pallas_call | solution.py:572

commit v6 on v5

--- a/solution.py
+++ b/solution.py
@@ -60,8 +60,11 @@
     small_dst,
     factor_buf,
     wkv,
+    left_buf,
+    right_buf,
     own_sem,
     wkv_sem,
+    pass_sem,
     small_send,
     small_recv,
     group_send,
@@ -208,8 +211,8 @@
 
     send_own(0)
     send_own(1)
-    loads[0].wait()
-    loads[1].wait()
+    for copy in loads[:2]:
+        copy.wait()
     scale = util[0] * (1.0 / math.sqrt(pop))
     weighted = nin[...].astype(F32) * scale
     out_factor = nout[...].astype(F32)
@@ -311,6 +314,11 @@
         def _(step):
             scores_of(step)
 
+    factor_copies = [
+        pltpu.make_async_copy(left_buf, left_out, pass_sem.at[0]),
+        pltpu.make_async_copy(right_buf, right_out, pass_sem.at[1]),
+    ]
+
     def update_part():
         for d in range(1, pop):
             origin = lax.rem(p + pop - d, pop)
@@ -322,9 +330,11 @@
         low = factor - high - mid
         factor_buf[...] = jnp.concatenate([high, mid, low], 0).T
         offset = pl.multiple_of(lax.rem(p * rows, LANES) if rows < LANES else 0, 8)
-        left_out[...] = factor_buf[pl.ds(offset, rows), :].astype(BF16)
+        left_buf[...] = factor_buf[pl.ds(offset, rows), :].astype(BF16)
         right = jnp.concatenate([small_dst[m, :, win : win + width] for m in range(pop)], 0)
-        right_out[...] = jnp.concatenate([right, right, right], 0).astype(BF16)
+        right_buf[...] = jnp.concatenate([right, right, right], 0).astype(BF16)
+        for copy in factor_copies:
+            copy.start()
 
     tile = 2 * LANES
     qxc, qyc, qdc = flip(qx, 1), flip(qy, 1), flip(qd, 1)
@@ -452,6 +462,10 @@
 
     factor = proj[...] * (SIGMA / math.sqrt(full))
 
+    def readout_copy(n):
+        lanes = pl.ds(pl.multiple_of(n * tile, tile), tile)
+        return pltpu.make_async_copy(wkv.at[0, :, lanes], wkv_hbm.at[0, :, lanes], wkv_sem.at[n])
+
     @pl.loop(0, width // tile)
     def _(n):
         lanes = pl.ds(pl.multiple_of(n * tile, tile), tile)
@@ -467,9 +481,8 @@
             here = pl.ds(pl.multiple_of(index * LANES, LANES), LANES)
             wkv[0, 0:half, here] = dot_nn(s_low[index], low_v).astype(BF16)
             wkv[0, half:length, here] = dot_nn(s_high[index], high_v).astype(BF16)
-
-    wkv_copy = pltpu.make_async_copy(wkv, wkv_hbm, wkv_sem)
-    wkv_copy.start()
+        readout_copy(n).start()
+
     for copy in sent:
         copy.wait_send()
     for s in range(tp - 1):
@@ -483,12 +496,21 @@
             def _():
                 up(s, c).wait_send()
 
-    wkv_copy.wait()
-
-
-def finish(wkv_in, left, right, wkv, upd, upd_buf, wkv_buf, sems, wkv_sem):
-    fetch = pltpu.make_async_copy(wkv_in, wkv_buf, wkv_sem.at[0])
-    fetch.start()
+    for n in range(width // tile):
+        readout_copy(n).wait()
+    for copy in factor_copies:
+        copy.wait()
+
+
+def finish(wkv_in, left_in, right_in, wkv, upd, upd_buf, wkv_buf, left, right, sems, load_sem, wkv_sem):
+    loads = [
+        pltpu.make_async_copy(src, dst, load_sem.at[i])
+        for i, (src, dst) in enumerate(((left_in, left), (right_in, right), (wkv_in, wkv_buf)))
+    ]
+    for copy in loads:
+        copy.start()
+    loads[0].wait()
+    loads[1].wait()
     count = sems.shape[0]
     size = upd_buf.shape[0] // count
     copies = []
@@ -499,8 +521,8 @@
         out.start()
         copies.append(out)
         if i == 0:
-            fetch.wait()
-            out = pltpu.make_async_copy(wkv_buf, wkv, wkv_sem.at[1])
+            loads[2].wait()
+            out = pltpu.make_async_copy(wkv_buf, wkv, wkv_sem)
             out.start()
             copies.append(out)
     for out in copies:
@@ -516,9 +538,8 @@
     half = length // 2
     group = pop // 8
     dma = pltpu.SemaphoreType.DMA
-    whole = pl.BlockSpec(memory_space=pltpu.VMEM)
+    hbm = pl.BlockSpec(memory_space=pltpu.HBM)
     scalar = pl.BlockSpec(memory_space=pltpu.SMEM)
-    hbm = pl.BlockSpec(memory_space=pltpu.HBM)
     wkv, left, right = pl.pallas_call(
         functools.partial(kernel, pop, tp),
         out_shape=(
@@ -527,7 +548,7 @@
             jax.ShapeDtypeStruct((3 * pop, width), BF16),
         ),
         in_specs=[hbm] * 7 + [scalar] * 2,
-        out_specs=(hbm, whole, whole),
+        out_specs=(hbm, hbm, hbm),
         scratch_shapes=[
             pltpu.VMEM((tp, length, width), BF16),
             pltpu.VMEM((full, width), BF16),
@@ -544,8 +565,11 @@
             pltpu.VMEM((pop, 1, win + width), F32),
             pltpu.VMEM((win, 3 * pop), F32),
             pltpu.VMEM((1, length, width), BF16),
+            pltpu.VMEM((rows, 3 * pop), BF16),
+            pltpu.VMEM((3 * pop, width), BF16),
             dma((7,)),
-            dma,
+            dma((width // (2 * LANES),)),
+            dma((2,)),
             dma((pop - 1,)),
             dma((pop - 1,)),
             dma((max(group - 1, 1),)),
@@ -575,9 +599,17 @@
             jax.ShapeDtypeStruct((1, length, width), BF16),
             jax.ShapeDtypeStruct((rows, width), F32),
         ),
-        in_specs=[hbm, whole, whole],
+        in_specs=[hbm] * 3,
         out_specs=(hbm, hbm),
-        scratch_shapes=[pltpu.VMEM((rows, width), F32), pltpu.VMEM((1, length, width), BF16), dma((tiles,)), dma((2,))],
+        scratch_shapes=[
+            pltpu.VMEM((rows, width), F32),
+            pltpu.VMEM((1, length, width), BF16),
+            pltpu.VMEM((rows, 3 * pop), BF16),
+            pltpu.VMEM((3 * pop, width), BF16),
+            dma((tiles,)),
+            dma((3,)),
+            dma,
+        ],
         compiler_params=pltpu.CompilerParams(vmem_limit_bytes=63 * 1024 * 1024),
     )(wkv, left, right)
 

time: 55.3 us -> 53.8 us (0.973)
  Pallas kernels: 53.2 us -> 51.7 us
    pallas_call x1, Pallas kernels: 49.8 us -> 49.1 us  [body(): pl.pallas_call(functools.partial(kernel, pop, tp), out_shape=(jax.ShapeDt...]
    pallas_call x1, Pallas kernels: 3.34 us -> 2.66 us  [body(): pl.pallas_call(finish, out_shape=(jax.ShapeDtypeStruct((1, length, width)...]
where the time goes in v6:
time: 53.8 us; the launch traced here: 53.7 us
  Pallas kernels  51.7 us (96%)
  between operations  1.93 us (4%)
    pallas_call x1, Pallas kernels, body(): pl.pallas_call(functools.partial(kernel, pop, tp), out_shape=(jax.ShapeDt...  49.1 us
    pallas_call x1, Pallas kernels, body(): pl.pallas_call(finish, out_shape=(jax.ShapeDtypeStruct((1, length, width)...  2.66 us

profile of v6, /device:TPU:1, one launch (start us, length us, event | category | flops | bytes accessed | tf_op | source)
XLA Modules:
  0.0 53.7 jit_solution(9368077965245540074)
XLA Ops:
  1.9 49.1 %shard_map.104 = (bf16[1,256,1024]{2,1,0:T(8,128)(2,1)}, bf16[512,24]{1,0:T(8,128)(2,1)}, bf16[24,1024]{1,0:T(8,128)(2,1)}) custom-call(bf16[1,256,1024]{2,1,0:T(8,128)(2,1)} %tok.1, bf16[1,256,1024]{2,1,0:T(8,128)(2,1)} %rec_hbm.1, bf16[1,256,1024]{2,1,0:T(8,128)(2,1)} %key_hbm.1, bf16[1,256,1024]{2,1,0:T(8,128)(2,1)} %dec_hbm.1, bf16[512,1024]{1,0:T(8,128)(2,1)} %w.1, ...), custom_call_target="tpu_custom_call" | custom-call | flops 2147483648 | bytes 16777216 | tf_op jit(solution)/shard_map/pallas_call | solution.py:543
  51.0 2.7 %shard_map.105 = (bf16[1,256,1024]{2,1,0:T(8,128)(2,1)}, f32[512,1024]{1,0:T(8,128)}) custom-call(bf16[1,256,1024]{2,1,0:T(8,128)(2,1)} %get-tuple-element.5.wkv_in, bf16[512,24]{1,0:T(8,128)(2,1)} %get-tuple-element.6.left_in, bf16[24,1024]{1,0:T(8,128)(2,1)} %get-tuple-element.7.right_in), custom_call_target="tpu_custom_call" | custom-call | tf_op jit(solution)/shard_map/pallas_call | solution.py:596

commit v7 on v6

--- a/solution.py
+++ b/solution.py
@@ -383,10 +383,9 @@
     start_tokens(0, 1)
     for i in range(WCUTS):
         send(own_piece(i), piece(q, i), c_send, c_recv, i, qc)
-    score_steps(0, share)
     send_own(2)
     send_own(3)
-    score_steps(share, 2 * share)
+    score_steps(0, 2 * share)
     take_tokens(0, 0)
     take_tokens(0, 1)
     round_of(0)

time: 53.8 us -> 53.8 us (level)
  no operation moved by 1% of the time
where the time goes in v7:
time: 53.8 us; the launch traced here: 53.7 us
  Pallas kernels  51.8 us (96%)
  between operations  1.93 us (4%)
    pallas_call x1, Pallas kernels, body(): pl.pallas_call(functools.partial(kernel, pop, tp), out_shape=(jax.ShapeDt...  49.1 us
    pallas_call x1, Pallas kernels, body(): pl.pallas_call(finish, out_shape=(jax.ShapeDtypeStruct((1, length, width)...  2.66 us

profile of v7, /device:TPU:1, one launch (start us, length us, event | category | flops | bytes accessed | tf_op | source)
XLA Modules:
  0.0 53.7 jit_solution(12743564236783162665)
XLA Ops:
  1.9 49.1 %shard_map.104 = (bf16[1,256,1024]{2,1,0:T(8,128)(2,1)}, bf16[512,24]{1,0:T(8,128)(2,1)}, bf16[24,1024]{1,0:T(8,128)(2,1)}) custom-call(bf16[1,256,1024]{2,1,0:T(8,128)(2,1)} %tok.1, bf16[1,256,1024]{2,1,0:T(8,128)(2,1)} %rec_hbm.1, bf16[1,256,1024]{2,1,0:T(8,128)(2,1)} %key_hbm.1, bf16[1,256,1024]{2,1,0:T(8,128)(2,1)} %dec_hbm.1, bf16[512,1024]{1,0:T(8,128)(2,1)} %w.1, ...), custom_call_target="tpu_custom_call" | custom-call | flops 2147483648 | bytes 16777216 | tf_op jit(solution)/shard_map/pallas_call | solution.py:542
  51.0 2.7 %shard_map.105 = (bf16[1,256,1024]{2,1,0:T(8,128)(2,1)}, f32[512,1024]{1,0:T(8,128)}) custom-call(bf16[1,256,1024]{2,1,0:T(8,128)(2,1)} %get-tuple-element.5.wkv_in, bf16[512,24]{1,0:T(8,128)(2,1)} %get-tuple-element.6.left_in, bf16[24,1024]{1,0:T(8,128)(2,1)} %get-tuple-element.7.right_in), custom_call_target="tpu_custom_call" | custom-call | tf_op jit(solution)/shard_map/pallas_call | solution.py:595
